TPU v7x, 256 devices: a whole 4x4x8 slice. The times are simulated.
256 devices in a mesh: row: 16 (over y, x_lo, core), col: 16 (over x_hi, z).
Axes of the slice: x: 4 (x_hi: 2, x_lo: 2; x = x_hi * 2 + x_lo), y: 4, z: 8, core: 2. Of those that a mesh axis runs over, the one named last changes fastest.
Arguments:
- feats: bfloat16 [32768, 2048], P(('row', 'col')), may hold values from -24 to 24
- weight: bfloat16 [2048, 512], replicated, may hold values from -0.125 to 0.125
- valid: int32 [32768], P(('row', 'col')), may hold values 0 or 1
Outputs:
- grad_embed: bfloat16 [32768, 512], P(('row', 'col'))
- grad_feats: bfloat16 [32768, 2048], P(('row', 'col'))
- grad_weight: float32 [2048, 512], P(('row', 'col'))
All inputs are finite; a program needn't handle non-finite values. No bound on the sum of `valid` on one device may be relied on, other than what follows from the above.
Results may differ from a plain program's by a relative error of at most 0.028.
Values may be sent and summed in bfloat16 or wider, within the bound.
A program may use at most 64 MiB of HBM per device.

v0:
```python
import math

import jax
import jax.numpy as jnp
from jax import lax
from jax.sharding import PartitionSpec as P


def local(feats, weight, valid):
    rows = feats.shape[0]
    feat_width = feats.shape[1]
    embed_width = weight.shape[1]
    n_row = lax.axis_size("row")
    n_col = lax.axis_size("col")
    frames = rows * n_row * n_col
    band_width = jnp.float32(embed_width // 4)
    embedding = jnp.dot(feats, weight, preferred_element_type=jnp.float32).astype(jnp.bfloat16)
    live = valid.astype(jnp.float32)
    live_half = live.astype(jnp.bfloat16)
    row_embed, row_flag = (
        lax.all_gather(embedding, "col", axis=0, tiled=True),
        lax.all_gather(live_half, "col", axis=0, tiled=True),
    )
    col_embed, col_flag = (
        lax.all_gather(embedding, "row", axis=0, tiled=True),
        lax.all_gather(live_half, "row", axis=0, tiled=True),
    )
    col_live = col_flag.astype(jnp.float32)
    row_wide = row_embed.astype(jnp.float32)
    row_norm = jnp.sum(row_wide * row_wide, axis=1)
    col_wide = col_embed.astype(jnp.float32)
    col_norm = jnp.sum(col_wide * col_wide, axis=1)
    total_rows = rows * n_col

    def kernel_tile(block, block_norm):
        inner = lax.dot_general(
            block, col_embed, (((1,), (1,)), ((), ())), preferred_element_type=jnp.float32
        )
        return jnp.exp(-(block_norm[:, None] + col_norm[None, :] - 2.0 * inner) / band_width)

    def mass_block(pieces):
        return jnp.sum(kernel_tile(pieces[0], pieces[1]) * col_live[None, :], axis=1)

    width = math.gcd(total_rows, 512)
    count = total_rows // width
    partial_mass = lax.map(
        mass_block, (row_embed.reshape(count, width, embed_width), row_norm.reshape(count, width))
    ).reshape(total_rows)
    own_mass = lax.psum_scatter(partial_mass, "col", scatter_dimension=0, tiled=True) + 1.0 - live
    row_mass = lax.all_gather(own_mass, "col", axis=0, tiled=True)
    col_mass = lax.all_gather(own_mass, "row", axis=0, tiled=True)
    row_inverse = 1.0 / row_mass
    col_inverse = 1.0 / col_mass
    block_norm = row_norm
    piece_width = math.gcd(rows * lax.axis_size("col"), 512)
    pieces = rows * lax.axis_size("col") // piece_width

    def one_block(parts):
        block, norm_part, inv_part = parts
        pair = (
            col_live[None, :]
            * (inv_part[:, None] + col_inverse[None, :])
            * kernel_tile(block, norm_part)
        ).astype(jnp.bfloat16)
        total = jnp.sum(pair.astype(jnp.float32), axis=1)
        return block.astype(jnp.float32) * total[:, None] - jnp.dot(
            pair, col_embed, preferred_element_type=jnp.float32
        )

    result = lax.map(
        one_block,
        (
            row_embed.reshape(pieces, piece_width, embed_width),
            block_norm.reshape(pieces, piece_width),
            row_inverse.reshape(pieces, piece_width),
        ),
    )
    pulled = lax.psum_scatter(
        result.reshape(rows * lax.axis_size("col"), embed_width).astype(jnp.bfloat16),
        "col",
        scatter_dimension=0,
        tiled=True,
    ).astype(jnp.float32)
    grad_embed = (0.5 * live[:, None] * pulled).astype(jnp.bfloat16)
    grad_feats = lax.dot_general(
        grad_embed, weight, (((1,), (1,)), ((), ())), preferred_element_type=jnp.float32
    ).astype(jnp.bfloat16)
    weight_term = lax.dot_general(
        feats, grad_embed, (((0,), (0,)), ((), ())), preferred_element_type=jnp.float32
    ) * jnp.float32(math.sqrt(feat_width) / frames)
    grad_weight = lax.psum_scatter(weight_term, ("row", "col"), scatter_dimension=0, tiled=True)
    return (grad_embed, grad_feats, grad_weight)


def solution(mesh):
    in_specs = (P(("row", "col"), None), P(), P(("row", "col")))
    out_specs = (P(("row", "col"), None), P(("row", "col"), None), P(("row", "col"), None))
    return jax.shard_map(local, mesh=mesh, in_specs=in_specs, out_specs=out_specs, check_vma=False)
```

profile of v0, /device:TPU:1, one launch (start us, length us, event | category | flops | bytes accessed | tf_op | source)
XLA Modules:
  0.0 1737.0 jit_solution(15238617600589161591)
XLA Ops:
  12.4 21.0 %all-gather = bf16[16,1,128]{2,1,0:T(2,128)(2,1)S(1)} all-gather(bf16[1,1,128]{2,1,0:T(2,128)(2,1)S(1)} %convert_bitcast_fusion), channel_id=1, replica_groups=mesh['row'=16,'col'=16] {'row'}, dimensions={0}, use_global_device_ids=true | all-gather | bytes 4352 | tf_op jit(solution)/shard_map/all_gather | solution.py:26
  35.3 61.6 %all-gather.6.cloned.1.call-done = bf16[2048,512]{1,0:T(8,128)(2,1)} async-done(((bf16[128,512]{1,0:T(8,128)(2,1)}), bf16[2048,512]{1,0:T(8,128)(2,1)}) %all-gather.6.cloned.1.call-update) | async-done | bytes 2097168 | tf_op jit(solution)/shard_map/all_gather | solution.py:21
  99.0 37.5 %all-gather.8.cloned.1.call-done = bf16[2048,512]{1,0:T(8,128)(2,1)} async-done(((bf16[128,512]{1,0:T(8,128)(2,1)}), bf16[2048,512]{1,0:T(8,128)(2,1)}) %all-gather.8.cloned.1.call-update) | async-done | bytes 2097168 | tf_op jit(solution)/shard_map/all_gather | solution.py:25
  138.6 14.3 while.20
  138.6 3.5 multiply_reduce_fusion.4
  142.2 3.5 multiply_reduce_fusion.4
  145.8 3.5 multiply_reduce_fusion.4
  149.3 3.5 multiply_reduce_fusion.4
  152.9 35.7 %all-reduce = f32[2048]{0:T(1024)S(1)} all-reduce(f32[2048]{0:T(1024)S(1)} %bitcast.70), channel_id=2, replica_groups=mesh['row'=16,'col'=16] {'col'}, use_global_device_ids=true, to_apply=%region_5.6.clone | all-reduce | flops 2048 | bytes 16384
  188.7 28.4 %all-gather.1 = f32[16,1,128]{2,1,0:T(1,128)S(1)} all-gather(f32[1,1,128]{2,1,0:T(1,128)S(1)} %get-tuple-element.132), channel_id=1, replica_groups=mesh['row'=16,'col'=16] {'col'}, dimensions={0}, use_global_device_ids=true | all-gather | bytes 8704 | tf_op jit(solution)/shard_map/all_gather | solution.py:50
  217.0 31.2 %all-gather.2 = f32[16,1,128]{2,1,0:T(1,128)S(1)} all-gather(f32[1,1,128]{2,1,0:T(1,128)S(1)} %get-tuple-element.132), channel_id=1, replica_groups=mesh['row'=16,'col'=16] {'row'}, dimensions={0}, use_global_device_ids=true | all-gather | bytes 8704 | tf_op jit(solution)/shard_map/all_gather | solution.py:51
  248.3 28.1 %while.21 = (s32[]{:T(128)}, bf16[4,512,512]{2,1,0:T(8,128)(2,1)}, bf16[4,512,512]{2,1,0:T(8,128)(2,1)}, f32[2048]{0:T(1024)S(1)}, f32[4,512]{1,0:T(4,128)S(1)},...) while((s32[]{:T(128)}, bf16[4,512,512]{2,1,0:T(8,128)(2,1)}, ...), condition=%wide.region_8.9_spmd, body=%wide.region_6.8_spmd.sunk | while | flops 2159803904 | bytes 18916484 | solution.py:70
  248.4 3.9 convert_reduce_fusion.2
  252.3 3.1 fusion.31
  255.4 3.9 convert_reduce_fusion.2
  259.3 3.1 fusion.31
  262.4 3.9 convert_reduce_fusion.2
  266.3 3.1 fusion.31
  269.4 3.9 convert_reduce_fusion.2
  273.3 3.1 fusion.31
  276.5 196.7 %reduce-scatter.5.cloned.1.call-done = bf16[128,512]{1,0:T(8,128)(2,1)} async-done(((bf16[2048,512]{1,0:T(8,128)(2,1)}), bf16[128,512]{1,0:T(8,128)(2,1)}) %reduce-scatter.5.cloned.1.call-update) | async-done | bytes 131088 | tf_op jit(solution)/shard_map/reduce_scatter | solution.py:78
  474.2 2.7 multiply_bitcast_fusion
  476.9 5.3 copy.8
  483.9 1246.6 %reduce-scatter.7.cloned.1.call-done = f32[8,512]{1,0:T(8,128)} async-done(((f32[2048,512]{1,0:T(8,128)}), f32[8,512]{1,0:T(8,128)}) %reduce-scatter.7.cloned.1.call-update) | async-done | bytes 16400
  (52 shorter events, 13.7 us)
Async XLA Ops:
  7.2 1.6 copy-start
  7.2 89.7 %all-gather.6.cloned.1.call-start = ((), (), s32[]{:S(2)}) async-start(), calls=%async_computation.2 | async-start | bytes 2228224 | tf_op jit(solution)/shard_map/all_gather | solution.py:21
  10.9 125.5 %all-gather.8.cloned.1.call-start = ((), (), s32[]{:S(2)}) async-start(), calls=%async_computation.3 | async-start | bytes 2228224 | tf_op jit(solution)/shard_map/all_gather | solution.py:25
  11.7 461.5 %reduce-scatter.5.cloned.1.call-start = ((), (), s32[]{:S(2)}) async-start(), calls=%async_computation.4 | async-start | bytes 2228224 | tf_op jit(solution)/shard_map/reduce_scatter | solution.py:78
  138.5 50.0 %copy-start.4 = (s32[128]{0:T(128)S(1)}, s32[128]{0:T(128)}, u32[]{:S(2)}) copy-start(s32[128]{0:T(128)} %param.9) | copy-start | bytes 1540
  248.3 225.9 %copy-start.2 = (bf16[128,2048]{1,0:T(8,128)(2,1)S(1)}, bf16[128,2048]{1,0:T(8,128)(2,1)}, u32[]{:S(2)}) copy-start(bf16[128,2048]{1,0:T(8,128)(2,1)} %param.7) | copy-start | bytes 1572868
  248.4 3.9 copy-start.1
  255.4 3.9 copy-start.1
  262.4 3.9 copy-start.1
  269.4 3.9 copy-start.1
  276.5 1454.0 %reduce-scatter.7.cloned.1.call-start = ((), (), s32[]{:S(2)}) async-start(), calls=%async_computation.5 | async-start | bytes 4210688
  474.2 8.0 copy-start.3
Sparse Core Ops, SparseCore 0:
  11.2 85.6 all-gather.5
  99.3 37.0 all-gather.7
  276.6 196.5 reduce-scatter.4
  482.4 1248.0 reduce-scatter.6
where the time goes:
time: 1770 us; the launch traced here: 1740 us
  waiting for transfers between devices  1540 us (87%)
  blocking collectives  116 us (7%)
  matrix products  48.4 us (3%)
    unnamed x5, waiting for transfers between devices  1250 us
    reduce_scatter x1, waiting for transfers between devices, local(): lax.psum_scatter(result.reshape(rows * lax.axis_size('col'), embed_width)...  197 us
    all_gather x1, waiting for transfers between devices, local(): lax.all_gather(embedding, 'col', axis=0, tiled=True)  61.6 us
    all_gather x1, waiting for transfers between devices, local(): lax.all_gather(embedding, 'row', axis=0, tiled=True)  37.5 us
    unnamed x1, blocking collectives  35.7 us
  transfers between devices with their start and end apart: 4, of which 4 were waited for; matrix products, arithmetic and copies ran while one was open for 0% of the time, Pallas kernels for 0%

commit v1 on v0

v1 whole, which is shorter than its diff:
```python
import functools
import math

import jax
import jax.numpy as jnp
from jax import lax
from jax.experimental import pallas as pl
from jax.experimental.pallas import tpu as pltpu
from jax.sharding import PartitionSpec as P

MESH = pl.DeviceIdType.MESH
XH, XL, Y, Z, C = 2, 2, 4, 8, 2
X = XH * XL
LINE = Z * C
PLANE = X * Y
FAR = 2.0**60


def device(x, y, z, k):
    return {"row": (y * XL + x % XL) * C + k, "col": (x // XL) * Z + z}


def to_row(column):
    n = column.shape[0]
    eye = lax.broadcasted_iota(jnp.int32, (n, n), 0) == lax.broadcasted_iota(jnp.int32, (n, n), 1)
    return jnp.sum(jnp.where(eye, column, 0.0), axis=0, keepdims=True)


def to_column(row):
    n = row.shape[1]
    eye = lax.broadcasted_iota(jnp.int32, (n, n), 0) == lax.broadcasted_iota(jnp.int32, (n, n), 1)
    return jnp.sum(jnp.where(eye, row, 0.0), axis=1, keepdims=True)


def nt(a, b):
    return lax.dot_general(a, b, (((1,), (1,)), ((), ())), preferred_element_type=jnp.float32)


def tn(a, b):
    return lax.dot_general(a, b, (((0,), (0,)), ((), ())), preferred_element_type=jnp.float32)


def kernel(
    feats, weight, valid,
    grad_embed, grad_feats, grad_weight,
    lines, planes, norms, tile, row_mass, row_masses, col_mass, col_masses,
    pulls, pulled, terms, term_in, parts, part_in,
    l_send, l_recv, q_send, q_recv, rm_send, rm_recv, cm_send, cm_recv,
    p_send, p_recv, t_send, t_recv, g_send, g_recv,
    *, band, scale,
):
    rows, embed = grad_embed.shape
    r, c = lax.axis_index("row"), lax.axis_index("col")
    k, x, y, z = r % C, (c // Z) * XL + (r // C) % XL, r // (C * XL), c % Z
    a = k * Z + z
    b = x * Y + y

    def line_mate(i):
        return device(x, y, i % Z, i // Z)

    def plane_mate(i):
        return device(i // Y, i % Y, z, k)

    barrier = pltpu.get_barrier_semaphore()

    def greet(d, carry):
        pl.semaphore_signal(barrier, inc=1, device_id=line_mate((a + d) % LINE), device_id_type=MESH)
        return carry

    def greet_plane(d, carry):
        pl.semaphore_signal(barrier, inc=1, device_id=plane_mate((b + d) % PLANE), device_id_type=MESH)
        return carry

    lax.fori_loop(1, LINE, greet, 0)
    lax.fori_loop(1, PLANE, greet_plane, 0)

    def at(ref, i, n):
        return ref.at[pl.ds(pl.multiple_of(i * n, n), n)]

    def copy(src, dst, send, recv, target):
        return pltpu.make_async_remote_copy(
            src_ref=src, dst_ref=dst, send_sem=send, recv_sem=recv, device_id=target, device_id_type=MESH
        )

    live_row = jnp.where(valid[...] > 0, 1.0, 0.0)
    live = to_column(live_row)
    embedding = jnp.dot(feats[...], weight[...], preferred_element_type=jnp.float32)
    away = jnp.where(lax.broadcasted_iota(jnp.int32, (rows, embed), 1) == 0, FAR, 0.0)
    own = jnp.where(live > 0.5, embedding, away).astype(jnp.bfloat16)
    at(lines, a, rows)[...] = own
    at(planes, b, rows)[...] = own

    pl.semaphore_wait(barrier, LINE + PLANE - 2)

    def line_copy(i, source):
        return copy(at(lines, a, rows), at(lines, source, rows), l_send.at[i], l_recv.at[source], line_mate(i))

    def plane_copy(i, source):
        return copy(at(planes, b, rows), at(planes, source, rows), q_send.at[i], q_recv.at[source], plane_mate(i))

    def over(n, me, action):
        def body(d, carry):
            action((me + d) % n)
            return carry

        lax.fori_loop(1, n, body, 0)

    over(LINE, a, lambda i: line_copy(i, a).start())
    over(PLANE, b, lambda i: plane_copy(i, b).start())
    over(LINE, a, lambda i: line_copy(i, i).wait_recv())
    over(PLANE, b, lambda i: plane_copy(i, i).wait_recv())

    def norm_step(i, carry):
        wide = at(planes, i, rows)[...].astype(jnp.float32)
        here = pl.ds(pl.multiple_of(i * rows, rows), rows)
        norms[0:1, here] = to_row(jnp.sum(wide * wide, axis=1, keepdims=True))
        return carry

    lax.fori_loop(0, PLANE, norm_step, 0)

    chunk = 2 * rows
    count = LINE // 2
    wide_columns = 512
    column_parts = PLANE * rows // wide_columns
    rate = -1.0 / (band * math.log(2.0))
    col_mass[...] = jnp.zeros_like(col_mass)

    def mass_step(i, carry):
        here = pl.ds(pl.multiple_of(i * chunk, chunk), chunk)
        block = lines[here, :]
        wide = block.astype(jnp.float32)
        norm = jnp.sum(wide * wide, axis=1, keepdims=True)
        twice = block * 2
        total = jnp.zeros((chunk, 1), jnp.float32)
        for j in range(column_parts):
            there = slice(j * wide_columns, (j + 1) * wide_columns)
            distance = (norm + norms[0:1, there]) - nt(twice, planes[there, :])
            value = jnp.exp2(distance * rate)
            tile[here, there] = value
            total = total + jnp.sum(value, axis=1, keepdims=True)
            col_mass[0:1, there] += jnp.sum(value, axis=0, keepdims=True)
        row_mass[pl.ds(i, 1), :] = to_row(total)
        return carry

    lax.fori_loop(0, count, mass_step, 0)

    def row_mass_copy(i, source):
        return copy(row_mass, row_masses.at[source], rm_send.at[i], rm_recv.at[source], line_mate(i))

    def col_mass_copy(i, source):
        return copy(col_mass, col_masses.at[source], cm_send.at[i], cm_recv.at[source], plane_mate(i))

    over(LINE, a, lambda i: row_mass_copy(i, a).start())
    over(PLANE, b, lambda i: col_mass_copy(i, b).start())
    row_masses[a] = row_mass[...]
    col_masses[b] = col_mass[...]
    over(LINE, a, lambda i: row_mass_copy(i, i).wait_recv())
    over(PLANE, b, lambda i: col_mass_copy(i, i).wait_recv())
    over(LINE, a, lambda i: row_mass_copy(i, i).wait_send())
    over(PLANE, b, lambda i: col_mass_copy(i, i).wait_send())
    row_mass[...] = 1.0 / jnp.sum(row_masses[...], axis=0)
    col_mass[...] = 1.0 / jnp.sum(col_masses[...], axis=0)

    def pull_copy(i, source):
        return copy(at(pulls, i, rows), at(pulled, source, rows), p_send.at[i], p_recv.at[source], line_mate(i))

    def pull_step(n, carry):
        i = (n + a // 2 + 1) % count
        here = pl.ds(pl.multiple_of(i * chunk, chunk), chunk)
        inverse = to_column(row_mass[pl.ds(i, 1), :])
        total = jnp.zeros((chunk, 1), jnp.float32)
        moved = jnp.zeros((chunk, embed), jnp.float32)
        for j in range(column_parts):
            there = slice(j * wide_columns, (j + 1) * wide_columns)
            pair = ((inverse + col_mass[0:1, there]) * tile[here, there]).astype(jnp.bfloat16)
            total = total + jnp.sum(pair.astype(jnp.float32), axis=1, keepdims=True)
            moved = moved + jnp.dot(pair, planes[there, :], preferred_element_type=jnp.float32)
        pulls[here, :] = (lines[here, :].astype(jnp.float32) * total - moved).astype(jnp.bfloat16)
        for m in range(2):

            @pl.when(2 * i + m != a)
            def _():
                pull_copy(2 * i + m, a).start()

        return carry

    lax.fori_loop(0, count, pull_step, 0)
    at(pulled, a, rows)[...] = at(pulls, a, rows)[...]
    over(LINE, a, lambda i: pull_copy(i, i).wait_recv())

    def add_pull(i, total):
        return total + at(pulled, i, rows)[...].astype(jnp.float32)

    pull = lax.fori_loop(0, LINE, add_pull, jnp.zeros((rows, embed), jnp.float32))
    gradient = jnp.where(live > 0.5, 0.5 * pull, 0.0).astype(jnp.bfloat16)
    grad_embed[...] = gradient

    natural = C * XH * Z * grad_weight.shape[0]
    share = Z * grad_weight.shape[0]
    for y_to in range(Y):
        for low in range(XL):
            start = (y_to * XL + low) * natural
            term = (tn(feats[:, start : start + natural], gradient) * scale).astype(jnp.bfloat16)
            for core in range(C):
                for high in range(XH):
                    to = (((high * XL + low) * Y + y_to) * C + core) * share
                    come = (core * XH + high) * share
                    terms[to : to + share, :] = term[come : come + share, :]
    slab = C * share

    def term_copy(i, source):
        return copy(at(terms, i, slab), at(term_in, source, slab), t_send.at[i], t_recv.at[source], plane_mate(i))

    over(PLANE, b, lambda i: term_copy(i, b).start())
    grad_feats[...] = nt(gradient, weight[...]).astype(jnp.bfloat16)
    at(term_in, b, slab)[...] = at(terms, b, slab)[...]
    over(PLANE, b, lambda i: term_copy(i, i).wait_recv())

    def add_term(i, total):
        return total + at(term_in, i, slab)[...].astype(jnp.float32)

    summed = lax.fori_loop(0, PLANE, add_term, jnp.zeros((slab, embed), jnp.float32))
    for i in range(LINE):
        parts[i] = summed[i * (slab // LINE) : (i + 1) * (slab // LINE), :]

    def part_copy(i, source):
        return copy(parts.at[i], part_in.at[source], g_send.at[i], g_recv.at[source], line_mate(i))

    over(LINE, a, lambda i: part_copy(i, a).start())
    part_in[a] = parts[a]
    over(LINE, a, lambda i: part_copy(i, i).wait_recv())
    grad_weight[...] = jnp.sum(part_in[...], axis=0)

    over(LINE, a, lambda i: line_copy(i, i).wait_send())
    over(PLANE, b, lambda i: plane_copy(i, i).wait_send())
    over(LINE, a, lambda i: pull_copy(i, i).wait_send())
    over(PLANE, b, lambda i: term_copy(i, i).wait_send())
    over(LINE, a, lambda i: part_copy(i, i).wait_send())


def local(feats, weight, valid):
    rows, width = feats.shape
    embed = weight.shape[1]
    devices = LINE * PLANE
    frames = rows * devices
    out_rows = width // devices
    half, single = jnp.bfloat16, jnp.float32
    vmem = pl.BlockSpec(memory_space=pltpu.VMEM)
    dma = pltpu.SemaphoreType.DMA
    return pl.pallas_call(
        functools.partial(
            kernel, band=float(embed // 4), scale=math.sqrt(width) / frames
        ),
        out_shape=(
            jax.ShapeDtypeStruct((rows, embed), half),
            jax.ShapeDtypeStruct((rows, width), half),
            jax.ShapeDtypeStruct((out_rows, embed), single),
        ),
        in_specs=[vmem] * 3,
        out_specs=(vmem,) * 3,
        scratch_shapes=[
            pltpu.VMEM((LINE * rows, embed), half),
            pltpu.VMEM((PLANE * rows, embed), half),
            pltpu.VMEM((1, PLANE * rows), single),
            pltpu.VMEM((LINE * rows, PLANE * rows), single),
            pltpu.VMEM((LINE // 2, 2 * rows), single),
            pltpu.VMEM((LINE, LINE // 2, 2 * rows), single),
            pltpu.VMEM((1, PLANE * rows), single),
            pltpu.VMEM((PLANE, 1, PLANE * rows), single),
            pltpu.VMEM((LINE * rows, embed), half),
            pltpu.VMEM((LINE * rows, embed), half),
            pltpu.VMEM((width, embed), half),
            pltpu.VMEM((width, embed), half),
            pltpu.VMEM((LINE, out_rows, embed), single),
            pltpu.VMEM((LINE, out_rows, embed), single),
        ]
        + [dma((LINE,)), dma((LINE,)), dma((PLANE,)), dma((PLANE,))] * 2
        + [dma((LINE,)), dma((LINE,)), dma((PLANE,)), dma((PLANE,)), dma((LINE,)), dma((LINE,))],
        compiler_params=pltpu.CompilerParams(
            collective_id=0, has_side_effects=True, vmem_limit_bytes=56 * 1024 * 1024
        ),
    )(feats, weight, valid.reshape(1, rows))


def solution(mesh):
    spec = P(("row", "col"), None)
    return jax.shard_map(
        local,
        mesh=mesh,
        in_specs=(spec, P(), P(("row", "col"))),
        out_specs=(spec, spec, spec),
        check_vma=False,
    )
```

time: 1770 us -> 183 us (0.10)
  the two profiles are of different devices: /device:TPU:1 before, /device:TPU:28 now
where the time goes in v1:
time: 183 us
  Pallas kernels  177 us (97%)
  local copies, waits for them, and re-layouts  4.77 us (3%)
    pallas_call x1, Pallas kernels, local(): pl.pallas_call(functools.partial(kernel, band=float(embed // 4), scale=ma...  177 us
    unnamed x3, local copies, waits for them, and re-layouts  4.77 us

profile of v1, /device:TPU:28, one launch (start us, length us, event | category | flops | bytes accessed | tf_op | source)
XLA Modules:
  0.0 182.6 jit_solution(14595656663263202990)
XLA Ops:
  0.6 177.2 %shard_map.58 = (bf16[128,512]{1,0:T(8,128)(2,1)}, bf16[128,2048]{1,0:T(8,128)(2,1)}, f32[8,512]{1,0:T(8,128)}) custom-call(bf16[128,2048]{1,0:T(8,128)(2,1)} %feats.1, bf16[2048,512]{1,0:T(8,128)(2,1)} %weight.1, s32[1,128]{1,0:T(1,128)} %bitcast.1), custom_call_target="tpu_custom_call" | custom-call | tf_op jit(solution)/shard_map/pallas_call | solution.py:250
  177.8 1.6 copy.9
  179.4 1.9 %copy.10 = bf16[128,2048]{1,0:T(8,128)(2,1)} copy(bf16[128,2048]{1,0:T(8,128)(2,1)} %get-tuple-element.7) | data formatting | bytes 1048576
  181.3 1.3 copy.11

commit v2 on v0

v2 whole, which is shorter than its diff:
```python
import functools
import math

import jax
import jax.numpy as jnp
from jax import lax
from jax.experimental import pallas as pl
from jax.experimental.pallas import tpu as pltpu
from jax.sharding import PartitionSpec as P

MESH = pl.DeviceIdType.MESH
XH, XL, Y, Z, C = 2, 2, 4, 8, 2
X = XH * XL
LINE = Z * C
PLANE = X * Y
FAR = 2.0**60
HALF, SINGLE = jnp.bfloat16, jnp.float32


def device(x, y, z, k):
    return {"row": (y * XL + x % XL) * C + k, "col": (x // XL) * Z + z}


def to_row(column):
    n = column.shape[0]
    eye = lax.broadcasted_iota(jnp.int32, (n, n), 0) == lax.broadcasted_iota(jnp.int32, (n, n), 1)
    return jnp.sum(jnp.where(eye, column, 0.0), axis=0, keepdims=True)


def to_column(row):
    n = row.shape[1]
    eye = lax.broadcasted_iota(jnp.int32, (n, n), 0) == lax.broadcasted_iota(jnp.int32, (n, n), 1)
    return jnp.sum(jnp.where(eye, row, 0.0), axis=1, keepdims=True)


def nt(a, b):
    return lax.dot_general(a, b, (((1,), (1,)), ((), ())), preferred_element_type=SINGLE)


def tn(a, b):
    return lax.dot_general(a, b, (((0,), (0,)), ((), ())), preferred_element_type=SINGLE)


class Gather:
    def __init__(self, send, recv):
        self.send, self.recv = send, recv
        self.made, self.arrived = {}, set()

    def add(self, name, make, needs=()):
        number = len(self.made)
        self.made[name] = (lambda mine: make(mine, self.send.at[number], self.recv.at[number])), needs

    def start(self, *names):
        for name in names:
            make, needs = self.made[name]
            for need in needs:
                self.wait(need)
            make(True).start()

    def wait(self, *names):
        for name in names:
            if name not in self.arrived:
                self.arrived.add(name)
                self.made[name][0](False).wait_recv()

    def finish(self):
        for name in self.made:
            self.made[name][0](True).wait_send()


def kernel(
    feats, weight, valid,
    grad_embed, grad_feats, grad_weight,
    lines, planes, norms, tile, row_mass, row_in, row_pair, row_ins, col_mass, col_ins, col_part, col_ins2,
    mine, sib_out, sib_in, run_out, run_in,
    mixed, leaving, gradients, first_out, first_in, second_out, second_in, third_out, third_in,
    g_send, g_recv, m_send, m_recv, s_send, s_recv, r_send, r_recv, w_send, w_recv,
    *, band, scale,
):
    rows, embed = grad_embed.shape
    r, c = lax.axis_index("row"), lax.axis_index("col")
    k, x, y, z = r % C, (c // Z) * XL + (r // C) % XL, r // (C * XL), c % Z
    sibling = device(x, y, z, 1 - k)

    def z_mate(d):
        return device(x, y, (z + d + Z) % Z, k)

    def x_mate(d):
        return device((x + d + X) % X, y, z, k)

    def y_mate(d):
        return device(x, (y + d + Y) % Y, z, k)

    barrier = pltpu.get_barrier_semaphore()
    friends = [sibling] + [z_mate(d) for d in range(1, Z)]
    friends += [x_mate(d) for d in range(1, X)] + [y_mate(d) for d in range(1, Y)]
    for friend in friends:
        pl.semaphore_signal(barrier, inc=1, device_id=friend, device_id_type=MESH)

    def span(start, n):
        return pl.ds(pl.multiple_of(start, n), n)

    def copy(src, dst, send, recv, target):
        return pltpu.make_async_remote_copy(
            src_ref=src, dst_ref=dst, send_sem=send, recv_sem=recv, device_id=target, device_id_type=MESH
        )

    live = to_column(jnp.where(valid[...] > 0, 1.0, 0.0))
    embedding = jnp.dot(feats[...], weight[...], preferred_element_type=SINGLE)
    away = jnp.where(lax.broadcasted_iota(jnp.int32, (rows, embed), 1) == 0, FAR, 0.0)
    own = jnp.where(live > 0.5, embedding, away).astype(HALF)
    lines[span((z * C + k) * rows, rows), :] = own
    planes[span((y * X + x) * rows, rows), :] = own
    group = XH * Z * grad_weight.shape[0]
    for g in range(Y * XL):
        low, high = feats[:, 2 * g * group : (2 * g + 1) * group], feats[:, (2 * g + 1) * group : (2 * g + 2) * group]
        here = slice(g * group, (g + 1) * group)
        mixed[0:rows, here] = jnp.where(k == 0, low, high)
        leaving[:, here] = jnp.where(k == 0, high, low)

    pl.semaphore_wait(barrier, len(friends))

    half, quarter = rows // 2, rows // 4
    gather = Gather(g_send, g_recv)

    def line_at(dz, core, start, n):
        return lines.at[span(((z + dz + Z) % Z * C + core) * rows + start, n)]

    def plane_at(dx, dy, start, n):
        return planes.at[span(((y + dy + Y) % Y * X + (x + dx + X) % X) * rows + start, n)]

    def along_z(s, d, h):
        def make(sender, send, recv):
            from_here = -s * (d - 1) if sender else -s * d
            ref = line_at(from_here, k, h * half, half)
            return copy(ref, ref, send, recv, z_mate(s))

        return make

    for s in (1, -1):
        for d in range(1, Z // 2 + 1):
            for h in (0, 1):
                if d < Z // 2 or h == (0 if s == 1 else 1):
                    gather.add(("z", s, d, h), along_z(s, d, h), [("z", s, d - 1, h)] if d > 1 else [])

    def across(o):
        def make(sender, send, recv):
            ref = line_at(o, k if sender else 1 - k, 0, rows)
            return copy(ref, ref, send, recv, sibling)

        return make

    for o in range(-Z // 2 + 1, Z // 2 + 1):
        if o == 0:
            needs = []
        elif o == Z // 2:
            needs = [("z", 1, o, 0), ("z", -1, o, 1)]
        else:
            needs = [("z", -1 if o > 0 else 1, abs(o), h) for h in (0, 1)]
        gather.add(("c", o), across(o), needs)

    def in_plane(axis, s, along, beside, start, n):
        def make(sender, send, recv):
            o = along if sender else along - s
            ref = plane_at(o, beside, start, n) if axis == "x" else plane_at(beside, o, start, n)
            return copy(ref, ref, send, recv, x_mate(s) if axis == "x" else y_mate(s))

        return make

    for axis, other, h in (("y", "x", 0), ("x", "y", 1)):
        for s in (1, -1):
            part = 0 if s == 1 else 1
            for g in (0, 1):
                gather.add((axis, s, "own", g), in_plane(axis, s, 0, 0, g * half, half))
            gather.add((axis, s, "far"), in_plane(axis, s, -s, 0, part * half, half), [(axis, s, "own", part)])
            for t in (1, -1):
                gather.add((axis, s, "side", t), in_plane(axis, s, 0, t, h * half, half), [(other, -t, "own", h)])
                gather.add(
                    (axis, s, "side far", t),
                    in_plane(axis, s, -s, t, h * half + part * quarter, quarter),
                    [(axis, s, "side", t)],
                )
            gather.add(
                (axis, s, "across"),
                in_plane(axis, s, 0, 2, h * half, half),
                [(other, 1 if h == 0 else -1, "far")],
            )
            gather.add(
                (axis, s, "across far"),
                in_plane(axis, s, -s, 2, h * half + part * quarter, quarter),
                [(axis, s, "across")],
            )

    def swap_copy(mine_, send, recv):
        return copy(leaving, mixed.at[span(rows, rows)], send, recv, sibling)

    gather.add("feats", swap_copy)

    both = (1, -1)
    gather.start(*[("x", s, "own", 0) for s in both], *[("y", s, "own", 1) for s in both])
    gather.start(*[("z", s, 1, 0) for s in both])
    gather.start(*[("x", s, "own", 1) for s in both], *[("y", s, "own", 0) for s in both])
    gather.start(*[("z", s, 1, 1) for s in both], ("c", 0), "feats")

    def norm_of(*offsets):
        for dx, dy in offsets:
            place = ((y + dy + Y) % Y * X + (x + dx + X) % X) * rows
            wide = planes[span(place, rows), :].astype(SINGLE)
            norms[0:1, span(place, rows)] = to_row(jnp.sum(wide * wide, axis=1, keepdims=True))

    norm_of((0, 0))
    gather.start(*[("z", s, 2, 0) for s in both], ("x", 1, "far"), ("y", -1, "far"))
    gather.start(*[(axis, s, "side", t) for t in both for axis in "yx" for s in both])
    gather.start(*[("z", s, 2, 1) for s in both], ("x", -1, "far"), ("y", 1, "far"), ("c", 1), ("c", -1))
    gather.wait(*[(axis, s, "own", g) for axis in "xy" for s in both for g in (0, 1)])
    norm_of((1, 0), (-1, 0), (0, 1), (0, -1))
    gather.start(*[("z", s, 3, 0) for s in both])
    gather.start(*[(axis, s, "across") for axis in "yx" for s in both])
    gather.start(*[(axis, s, "side far", t) for t in both for axis in "yx" for s in both])
    gather.start(*[("z", s, 3, 1) for s in both], ("c", 2), ("c", -2))
    gather.start(("z", 1, 4, 0), ("z", -1, 4, 1))
    gather.start(*[(axis, s, "across far") for axis in "yx" for s in both])
    gather.wait(*[(axis, s, "side", t) for axis in "xy" for s in both for t in both])
    gather.wait(*[(axis, s, "far") for axis in "xy" for s in both])
    norm_of((1, 1), (1, -1), (-1, 1), (-1, -1), (2, 0), (0, 2))
    gather.start(("c", 3), ("c", -3), ("c", 4))
    gather.wait(*gather.made)
    norm_of((2, 1), (2, -1), (1, 2), (-1, 2), (2, 2))

    chunk = C * rows
    tall, wide_columns = 2 * chunk, chunk
    rate = -1.0 / (band * math.log(2.0))
    col_mass[...] = jnp.zeros_like(col_mass)

    def mass_step(i, carry):
        here = span(i * tall, tall)
        block = lines[here, :]
        wide = block.astype(SINGLE)
        norm = jnp.sum(wide * wide, axis=1, keepdims=True)
        twice = block * 2
        total = jnp.zeros((tall, 1), SINGLE)
        for j in range(PLANE * rows // wide_columns):
            there = slice(j * wide_columns, (j + 1) * wide_columns)
            distance = (norm + norms[0:1, there]) - nt(twice, planes[there, :])
            value = jnp.exp2(distance * rate)
            tile[here, there] = value
            total = total + jnp.sum(value, axis=1, keepdims=True)
            col_mass[0:1, there] += jnp.sum(value, axis=0, keepdims=True)
        for j in range(2):
            row_mass[pl.ds(2 * i + j, 1), :] = to_row(total[j * chunk : (j + 1) * chunk, :])
        return carry

    lax.fori_loop(0, Z // 2, mass_step, 0)

    mass = Gather(m_send, m_recv)
    mass.add("c", lambda mine_, send, recv: copy(row_mass, row_in, send, recv, sibling))

    def direct(source, target, mate, size, at, d):
        def make(sender, send, recv):
            return copy(source, target.at[at if sender else (at - d + size) % size], send, recv, mate(d))

        return make

    for d in range(1, X):
        mass.add(("x", d), direct(col_mass, col_ins, x_mate, X, x, d))
    for d in range(1, Y):
        mass.add(("y", d), direct(col_part, col_ins2, y_mate, Y, y, d))
    for d in range(1, Z):
        mass.add(("z", d), direct(row_pair, row_ins, z_mate, Z, z, d))
    mass.start("c", *[("x", d) for d in range(1, X)])
    col_ins[x] = col_mass[...]
    mass.wait("c")
    row_pair[...] = row_mass[...] + row_in[...]
    mass.start(*[("z", d) for d in range(1, Z)])
    row_ins[z] = row_pair[...]
    mass.wait(*[("x", d) for d in range(1, X)])
    col_part[...] = jnp.sum(col_ins[...], axis=0)
    mass.start(*[("y", d) for d in range(1, Y)])
    col_ins2[y] = col_part[...]
    mass.wait(*mass.made)
    mass.finish()
    row_mass[...] = 1.0 / jnp.sum(row_ins[...], axis=0)
    col_mass[...] = 1.0 / jnp.sum(col_ins2[...], axis=0)

    def pair_copy(n):
        return copy(sib_out.at[n], sib_in.at[n], s_send.at[n], s_recv.at[n], sibling)

    def run_copy(s, m, h):
        here = pl.ds(h * half, half)
        at = (s * 4 + m) * 2 + h
        return copy(
            run_out.at[s * 4 + m, here], run_in.at[s * 4 + m, here], r_send.at[at], r_recv.at[at], z_mate(2 * s - 1)
        )

    run_in[4, half:rows, :] = jnp.zeros((half, embed), HALF)
    run_in[0, 0:half, :] = jnp.zeros((half, embed), HALF)

    def link(i):
        m, s = (i + 1) // 2, i % 2
        pair_copy(i).wait_recv()
        for h in (0, 1):
            here = slice(h * half, (h + 1) * half)

            @pl.when(jnp.logical_or(m > 1, s == 1 - h))
            def _():
                run_copy(s, m - 1, h).wait_recv()

            total = mine[i, here, :] + sib_in[i, here, :].astype(SINGLE) + run_in[s * 4 + m - 1, here, :].astype(SINGLE)
            run_out[s * 4 + m, here, :] = total.astype(HALF)
            run_copy(s, m, h).start()

    def pull_step(n, carry):
        o = (4 - (n + 1) // 2) * (2 * (n % 2) - 1)
        i = (z + o + Z) % Z
        here = span(i * chunk, chunk)
        inverse = to_column(row_mass[pl.ds(i, 1), :])
        total = jnp.zeros((chunk, 1), SINGLE)
        moved = jnp.zeros((chunk, embed), SINGLE)
        width = 2 * chunk
        for j in range(PLANE * rows // width):
            there = slice(j * width, (j + 1) * width)
            pair = ((inverse + col_mass[0:1, there]) * tile[here, there]).astype(HALF)
            total = total + jnp.sum(pair.astype(SINGLE), axis=1, keepdims=True)
            moved = moved + jnp.dot(pair, planes[there, :], preferred_element_type=SINGLE)
        pull = lines[here, :].astype(SINGLE) * total - moved
        mine[n] = jnp.where(k == 0, pull[0:rows, :], pull[rows:chunk, :])
        sib_out[n] = jnp.where(k == 0, pull[rows:chunk, :], pull[0:rows, :]).astype(HALF)
        pair_copy(n).start()

        @pl.when(n == 1)
        def _():
            pair_copy(0).wait_recv()
            far = (mine[0] + sib_in[0].astype(SINGLE)).astype(HALF)
            run_out[4] = far
            run_out[0] = far
            run_copy(1, 0, 0).start()
            run_copy(0, 0, 1).start()

        @pl.when(n >= 2)
        def _():
            link(n - 1)

        return carry

    lax.fori_loop(0, Z, pull_step, 0)
    pair_copy(Z - 1).wait_recv()
    pull = mine[Z - 1] + sib_in[Z - 1].astype(SINGLE)
    for s in (0, 1):
        for h in (0, 1):
            run_copy(s, 3, h).wait_recv()
        pull = pull + run_in[s * 4 + 3].astype(SINGLE)
    gradient = jnp.where(live > 0.5, 0.5 * pull, 0.0).astype(HALF)

    gradients[0:rows, :] = gradient
    terms = Gather(w_send, w_recv)
    terms.add("c", lambda mine_, send, recv: copy(gradients.at[span(0, rows)], gradients.at[span(rows, rows)], send, recv, sibling))
    terms.start("c")
    grad_embed[...] = gradient
    gather.wait("feats")
    split = embed // 2
    share = group // XH

    def first(table, axis, mate, size, at, d):
        def make(sender, send, recv):
            return copy(
                first_out.at[table, (at + d) % size],
                first_in.at[table, at if sender else (at - d + size) % size],
                send, recv, mate(d),
            )

        return make

    def second(table, mate, size, at, d):
        def make(sender, send, recv):
            return copy(
                second_out.at[table, (at + d) % size],
                second_in.at[table, at if sender else (at - d + size) % size],
                send, recv, mate(d),
            )

        return make

    def third(d):
        def make(sender, send, recv):
            return copy(third_out.at[(z + d) % Z], third_in.at[z if sender else (z - d + Z) % Z], send, recv, z_mate(d))

        return make

    for d in range(1, X):
        terms.add(("first", 0, d), first(0, "x", x_mate, X, x, d))
        terms.add(("second", 1, d), second(1, x_mate, X, x, d))
    for d in range(1, Y):
        terms.add(("first", 1, d), first(1, "y", y_mate, Y, y, d))
        terms.add(("second", 0, d), second(0, y_mate, Y, y, d))
    for d in range(1, Z):
        terms.add(("third", d), third(d))

    terms.wait("c")
    both_gradients = gradients[...]
    for g in range(Y * XL):
        to_y, low = g // XL, g % XL
        term = (tn(mixed[:, g * group : (g + 1) * group], both_gradients) * scale).astype(HALF)
        for high in range(XH):
            to_x = high * XL + low
            piece = term[high * share : (high + 1) * share, :]
            first_out[0, to_x, to_y * share : (to_y + 1) * share, :] = piece[:, 0:split]
            first_out[1, to_y, to_x * share : (to_x + 1) * share, :] = piece[:, split:embed]
    for d in range(1, X):
        terms.start(("first", 0, d), ("first", 1, d))
    grad_feats[...] = nt(gradient, weight[...]).astype(HALF)
    for table, at in ((0, x), (1, y)):
        first_in[table, at] = first_out[table, at]
        terms.wait(*[("first", table, d) for d in range(1, X)])
        added = jnp.sum(first_in[table].astype(SINGLE), axis=0).astype(HALF)
        for i in range(4):
            second_out[table, i] = added[i * share : (i + 1) * share, :]
        terms.start(*[("second", table, d) for d in range(1, X)])
    for table, at in ((0, y), (1, x)):
        second_in[table, at] = second_out[table, at]
        terms.wait(*[("second", table, d) for d in range(1, X)])
        added = jnp.sum(second_in[table].astype(SINGLE), axis=0)
        for i in range(Z):
            third_out[i, :, table * split : (table + 1) * split] = added[i * (share // Z) : (i + 1) * (share // Z), :]
    terms.start(*[("third", d) for d in range(1, Z)])
    third_in[z] = third_out[z]
    terms.wait(*terms.made)
    grad_weight[...] = jnp.sum(third_in[...], axis=0)

    gather.finish()
    terms.finish()
    for n in range(Z):
        pair_copy(n).wait_send()
    run_copy(1, 0, 0).wait_send()
    run_copy(0, 0, 1).wait_send()
    for s in (0, 1):
        for m in (1, 2, 3):
            for h in (0, 1):
                run_copy(s, m, h).wait_send()


def local(feats, weight, valid):
    rows, width = feats.shape
    embed = weight.shape[1]
    frames = rows * LINE * PLANE
    out_rows = width // (LINE * PLANE)
    vmem = pl.BlockSpec(memory_space=pltpu.VMEM)

    def half(*shape):
        return pltpu.VMEM(shape, HALF)

    def single(*shape):
        return pltpu.VMEM(shape, SINGLE)

    def dma(n):
        return [pltpu.SemaphoreType.DMA((n,))] * 2

    share = Z * out_rows
    columns = PLANE * rows
    return pl.pallas_call(
        functools.partial(kernel, band=float(embed // 4), scale=math.sqrt(width) / frames),
        out_shape=(
            jax.ShapeDtypeStruct((rows, embed), HALF),
            jax.ShapeDtypeStruct((rows, width), HALF),
            jax.ShapeDtypeStruct((out_rows, embed), SINGLE),
        ),
        in_specs=[vmem] * 3,
        out_specs=(vmem,) * 3,
        scratch_shapes=[
            half(LINE * rows, embed), half(columns, embed), single(1, columns), single(LINE * rows, columns),
            single(Z, C * rows), single(Z, C * rows), single(Z, C * rows), single(Z, Z, C * rows),
            single(1, columns), single(X, 1, columns), single(1, columns), single(Y, 1, columns),
            single(Z, rows, embed), half(Z, rows, embed), half(Z, rows, embed),
            half(8, rows, embed), half(8, rows, embed),
            half(2 * rows, width // 2), half(rows, width // 2), half(2 * rows, embed),
            half(2, 4, 4 * share, embed // 2), half(2, 4, 4 * share, embed // 2),
            half(2, 4, share, embed // 2), half(2, 4, share, embed // 2),
            single(Z, out_rows, embed), single(Z, out_rows, embed),
        ]
        + dma(64) + dma(14) + dma(Z) + dma(16) + dma(20),
        compiler_params=pltpu.CompilerParams(
            collective_id=0, has_side_effects=True, vmem_limit_bytes=56 * 1024 * 1024
        ),
    )(feats, weight, valid.reshape(1, rows))


def solution(mesh):
    spec = P(("row", "col"), None)
    return jax.shard_map(
        local,
        mesh=mesh,
        in_specs=(spec, P(), P(("row", "col"))),
        out_specs=(spec, spec, spec),
        check_vma=False,
    )
```

time: 1770 us -> 90 us (0.05); the launches traced: 1740 us -> 89.8 us
  waiting for transfers between devices: 1540 us -> 0 us
  blocking collectives: 116 us -> 0 us
  Pallas kernels: 0 us -> 84.4 us
  matrix products: 48.4 us -> 0 us
    unnamed x5 -> x0, waiting for transfers between devices: 1250 us -> none
    reduce_scatter x1 -> x0, waiting for transfers between devices: 197 us -> none  [local(): lax.psum_scatter(result.reshape(rows * lax.axis_size('col'), embed_width)...]
    all_gather x2 -> x0, waiting for transfers between devices: 99 us -> none  [the longest x1 61.6 us: local(): lax.all_gather(embedding, 'col', axis=0, tiled=True)]
    pallas_call x0 -> x1, Pallas kernels: none -> 84.4 us  [local(): pl.pallas_call(functools.partial(kernel, band=float(embed // 4), scale=ma...]
    all_gather x3 -> x0, blocking collectives: 80.6 us -> none  [the longest x1 31.2 us: local(): col_mass = lax.all_gather(own_mass, 'row', axis=0, tiled=True)]
    dot_general x15 -> x0, matrix products: 48.4 us -> none  [the longest x8 29.6 us: kernel_tile(): lax.dot_general(block, col_embed, (((1,), (1,)), ((), ())), preferred_ele...]
    unnamed x1 -> x0, blocking collectives: 35.7 us -> none
  transfers between devices with their start and end apart: 4 -> 0, of which waited for: 4 -> 0; matrix products, arithmetic and copies ran while one was open for 0% -> 0% of each run, Pallas kernels for 0% -> 0%
where the time goes in v2:
time: 90 us; the launch traced here: 89.8 us
  Pallas kernels  84.4 us (94%)
  local copies, waits for them, and re-layouts  4.77 us (5%)
    pallas_call x1, Pallas kernels, local(): pl.pallas_call(functools.partial(kernel, band=float(embed // 4), scale=ma...  84.4 us
    unnamed x3, local copies, waits for them, and re-layouts  4.77 us

profile of v2, /device:TPU:1, one launch (start us, length us, event | category | flops | bytes accessed | tf_op | source)
XLA Modules:
  0.0 89.8 jit_solution(17598233571934189985)
XLA Ops:
  0.6 84.4 %shard_map.58 = (bf16[128,512]{1,0:T(8,128)(2,1)}, bf16[128,2048]{1,0:T(8,128)(2,1)}, f32[8,512]{1,0:T(8,128)}) custom-call(bf16[128,2048]{1,0:T(8,128)(2,1)} %feats.1, bf16[2048,512]{1,0:T(8,128)(2,1)} %weight.1, s32[1,128]{1,0:T(1,128)} %bitcast.1), custom_call_target="tpu_custom_call" | custom-call | tf_op jit(solution)/shard_map/pallas_call | solution.py:459
  85.0 1.6 %copy.9 = bf16[128,512]{1,0:T(8,128)(2,1)} copy(bf16[128,512]{1,0:T(8,128)(2,1)} %get-tuple-element.6) | data formatting | bytes 262144
  86.6 1.9 %copy.10 = bf16[128,2048]{1,0:T(8,128)(2,1)} copy(bf16[128,2048]{1,0:T(8,128)(2,1)} %get-tuple-element.7) | data formatting | bytes 1048576
  88.5 1.3 %copy.11 = f32[8,512]{1,0:T(8,128)} copy(f32[8,512]{1,0:T(8,128)} %get-tuple-element.8) | data formatting | bytes 32768

commit v3 on v2

--- a/solution.py
+++ b/solution.py
@@ -14,7 +14,20 @@
 LINE = Z * C
 PLANE = X * Y
 FAR = 2.0**60
+ALONG = (0, 1, -1, 2, -2, 3, -3, 4)
+AROUND = (
+    (0, 0), (1, 0), (-1, 0), (0, 1), (0, -1), (2, 0), (0, 2), (1, 1), (-1, 1), (1, -1), (-1, -1),
+    (2, 1), (2, -1), (1, 2), (-1, 2), (2, 2),
+)
 HALF, SINGLE = jnp.bfloat16, jnp.float32
+
+
+def line_slot(dz):
+    return ALONG.index((dz + Z // 2 - 1) % Z - Z // 2 + 1)
+
+
+def plane_slot(dx, dy):
+    return AROUND.index(((dx + 1) % X - 1, (dy + 1) % Y - 1))
 
 
 def device(x, y, z, k):
@@ -69,12 +82,14 @@
 
 
 def kernel(
-    feats, weight, valid,
+    feats_in, weight_in, valid_in,
     grad_embed, grad_feats, grad_weight,
-    lines, planes, norms, tile, row_mass, row_in, row_pair, row_ins, col_mass, col_ins, col_part, col_ins2,
+    feats, weight, valid, embed_out, feats_out, weight_out,
+    lines, planes, norms, tile, row_norm, row_sum, col_sum,
+    row_mass, row_in, row_pair, row_ins, col_mass, col_ins, col_part, col_ins2,
     mine, sib_out, sib_in, run_out, run_in,
     mixed, leaving, gradients, first_out, first_in, second_out, second_in, third_out, third_in,
-    g_send, g_recv, m_send, m_recv, s_send, s_recv, r_send, r_recv, w_send, w_recv,
+    load, store, g_send, g_recv, m_send, m_recv, s_send, s_recv, r_send, r_recv, w_send, w_recv,
     *, band, scale,
 ):
     rows, embed = grad_embed.shape
@@ -97,6 +112,20 @@
     for friend in friends:
         pl.semaphore_signal(barrier, inc=1, device_id=friend, device_id_type=MESH)
 
+    depth = weight.shape[0] // 4
+    loads = [
+        pltpu.make_async_copy(valid_in, valid, load.at[0]),
+        pltpu.make_async_copy(feats_in, feats, load.at[1]),
+    ]
+    for i in range(4):
+        part = pl.ds(i * depth, depth)
+        loads.append(pltpu.make_async_copy(weight_in.at[part], weight.at[part], load.at[2 + i]))
+    for one in loads:
+        one.start()
+    col_sum[...] = jnp.zeros_like(col_sum)
+    loads[0].wait()
+    loads[1].wait()
+
     def span(start, n):
         return pl.ds(pl.multiple_of(start, n), n)
 
@@ -106,11 +135,15 @@
         )
 
     live = to_column(jnp.where(valid[...] > 0, 1.0, 0.0))
-    embedding = jnp.dot(feats[...], weight[...], preferred_element_type=SINGLE)
+    embedding = jnp.zeros((rows, embed), SINGLE)
+    for i in range(4):
+        loads[2 + i].wait()
+        part = slice(i * depth, (i + 1) * depth)
+        embedding = embedding + jnp.dot(feats[:, part], weight[part, :], preferred_element_type=SINGLE)
     away = jnp.where(lax.broadcasted_iota(jnp.int32, (rows, embed), 1) == 0, FAR, 0.0)
     own = jnp.where(live > 0.5, embedding, away).astype(HALF)
-    lines[span((z * C + k) * rows, rows), :] = own
-    planes[span((y * X + x) * rows, rows), :] = own
+    lines[span(k * rows, rows), :] = own
+    planes[0:rows, :] = own
     group = XH * Z * grad_weight.shape[0]
     for g in range(Y * XL):
         low, high = feats[:, 2 * g * group : (2 * g + 1) * group], feats[:, (2 * g + 1) * group : (2 * g + 2) * group]
@@ -124,16 +157,15 @@
     gather = Gather(g_send, g_recv)
 
     def line_at(dz, core, start, n):
-        return lines.at[span(((z + dz + Z) % Z * C + core) * rows + start, n)]
+        return lines.at[span((line_slot(dz) * C + core) * rows + start, n)]
 
     def plane_at(dx, dy, start, n):
-        return planes.at[span(((y + dy + Y) % Y * X + (x + dx + X) % X) * rows + start, n)]
+        return planes.at[pl.ds(plane_slot(dx, dy) * rows + start, n)]
 
     def along_z(s, d, h):
         def make(sender, send, recv):
-            from_here = -s * (d - 1) if sender else -s * d
-            ref = line_at(from_here, k, h * half, half)
-            return copy(ref, ref, send, recv, z_mate(s))
+            source = line_at(-s * (d - 1), k, h * half, half)
+            return copy(source, line_at(-s * d, k, h * half, half), send, recv, z_mate(s))
 
         return make
 
@@ -161,9 +193,11 @@
 
     def in_plane(axis, s, along, beside, start, n):
         def make(sender, send, recv):
-            o = along if sender else along - s
-            ref = plane_at(o, beside, start, n) if axis == "x" else plane_at(beside, o, start, n)
-            return copy(ref, ref, send, recv, x_mate(s) if axis == "x" else y_mate(s))
+            if axis == "x":
+                source, target = plane_at(along, beside, start, n), plane_at(along - s, beside, start, n)
+                return copy(source, target, send, recv, x_mate(s))
+            source, target = plane_at(beside, along, start, n), plane_at(beside, along - s, start, n)
+            return copy(source, target, send, recv, y_mate(s))
 
         return make
 
@@ -202,55 +236,86 @@
     gather.start(*[("x", s, "own", 1) for s in both], *[("y", s, "own", 0) for s in both])
     gather.start(*[("z", s, 1, 1) for s in both], ("c", 0), "feats")
 
-    def norm_of(*offsets):
-        for dx, dy in offsets:
-            place = ((y + dy + Y) % Y * X + (x + dx + X) % X) * rows
-            wide = planes[span(place, rows), :].astype(SINGLE)
-            norms[0:1, span(place, rows)] = to_row(jnp.sum(wide * wide, axis=1, keepdims=True))
-
-    norm_of((0, 0))
+    def norm_of(first, last):
+        for i in range(first, last):
+            here = slice(i * rows, (i + 1) * rows)
+            wide = planes[here, :].astype(SINGLE)
+            norms[0:1, here] = to_row(jnp.sum(wide * wide, axis=1, keepdims=True))
+
+    chunk = C * rows
+    rate = -1.0 / (band * math.log(2.0))
+
+    def work(first_row, last_row, first_unit, last_unit):
+        def step(i, carry):
+            here = span(i * chunk, chunk)
+            block = lines[here, :]
+            if first_unit == 0:
+                wide = block.astype(SINGLE)
+                norm = jnp.broadcast_to(jnp.sum(wide * wide, axis=1, keepdims=True), (chunk, 128))
+                row_norm[here, :] = norm
+                total = jnp.zeros((chunk, 128), SINGLE)
+            else:
+                norm = row_norm[here, :]
+                total = row_sum[here, :]
+            norm = jnp.concatenate([norm] * (chunk // 128), axis=1)
+            twice = block * 2
+            for j in range(first_unit, last_unit):
+                there = slice(j * chunk, (j + 1) * chunk)
+                distance = (norm + norms[0:1, there]) - nt(twice, planes[there, :])
+                value = jnp.exp2(distance * rate)
+                tile[here, there] = value
+                for p in range(chunk // 128):
+                    total = total + value[:, p * 128 : (p + 1) * 128]
+                col_sum[:, there] += jnp.sum(value.reshape(chunk // 8, 8, chunk), axis=0)
+            row_sum[here, :] = total
+            return carry
+
+        lax.fori_loop(first_row, last_row, step, 0)
+
+    norm_of(0, 1)
     gather.start(*[("z", s, 2, 0) for s in both], ("x", 1, "far"), ("y", -1, "far"))
     gather.start(*[(axis, s, "side", t) for t in both for axis in "yx" for s in both])
     gather.start(*[("z", s, 2, 1) for s in both], ("x", -1, "far"), ("y", 1, "far"), ("c", 1), ("c", -1))
     gather.wait(*[(axis, s, "own", g) for axis in "xy" for s in both for g in (0, 1)])
-    norm_of((1, 0), (-1, 0), (0, 1), (0, -1))
+    norm_of(1, 5)
+    gather.wait(("c", 0), ("c", 1), ("c", -1))
+    work(0, 3, 0, 2)
     gather.start(*[("z", s, 3, 0) for s in both])
     gather.start(*[(axis, s, "across") for axis in "yx" for s in both])
     gather.start(*[(axis, s, "side far", t) for t in both for axis in "yx" for s in both])
     gather.start(*[("z", s, 3, 1) for s in both], ("c", 2), ("c", -2))
+    gather.wait(*[(axis, s, "far") for axis in "xy" for s in both])
+    norm_of(5, 11)
+    work(0, 3, 2, 5)
     gather.start(("z", 1, 4, 0), ("z", -1, 4, 1))
     gather.start(*[(axis, s, "across far") for axis in "yx" for s in both])
-    gather.wait(*[(axis, s, "side", t) for axis in "xy" for s in both for t in both])
-    gather.wait(*[(axis, s, "far") for axis in "xy" for s in both])
-    norm_of((1, 1), (1, -1), (-1, 1), (-1, -1), (2, 0), (0, 2))
+    gather.wait(("c", 2), ("c", -2))
+    work(3, 5, 0, 5)
     gather.start(("c", 3), ("c", -3), ("c", 4))
+    gather.wait(*[(axis, s, "side far", t) for t in both for axis in "yx" for s in both])
+    norm_of(11, 15)
+    work(0, 5, 5, 7)
+    gather.wait(("c", 3), ("c", -3))
+    work(5, 7, 0, 7)
     gather.wait(*gather.made)
-    norm_of((2, 1), (2, -1), (1, 2), (-1, 2), (2, 2))
-
-    chunk = C * rows
-    tall, wide_columns = 2 * chunk, chunk
-    rate = -1.0 / (band * math.log(2.0))
-    col_mass[...] = jnp.zeros_like(col_mass)
-
-    def mass_step(i, carry):
-        here = span(i * tall, tall)
-        block = lines[here, :]
-        wide = block.astype(SINGLE)
-        norm = jnp.sum(wide * wide, axis=1, keepdims=True)
-        twice = block * 2
-        total = jnp.zeros((tall, 1), SINGLE)
-        for j in range(PLANE * rows // wide_columns):
-            there = slice(j * wide_columns, (j + 1) * wide_columns)
-            distance = (norm + norms[0:1, there]) - nt(twice, planes[there, :])
-            value = jnp.exp2(distance * rate)
-            tile[here, there] = value
-            total = total + jnp.sum(value, axis=1, keepdims=True)
-            col_mass[0:1, there] += jnp.sum(value, axis=0, keepdims=True)
-        for j in range(2):
-            row_mass[pl.ds(2 * i + j, 1), :] = to_row(total[j * chunk : (j + 1) * chunk, :])
+    norm_of(15, 16)
+    work(0, 7, 7, 8)
+    work(7, 8, 0, 8)
+
+    def row_total(i, carry):
+        place = (z + (i + 1) // 2 * (2 * (i % 2) - 1) + Z) % Z
+        row_mass[pl.ds(place, 1), :] = to_row(jnp.sum(row_sum[span(i * chunk, chunk), :], axis=1, keepdims=True))
         return carry
 
-    lax.fori_loop(0, Z // 2, mass_step, 0)
+    lax.fori_loop(0, Z, row_total, 0)
+
+    def absolute(slot):
+        dx, dy = AROUND[slot]
+        return span(((y + dy + Y) % Y * X + (x + dx + X) % X) * rows, rows)
+
+    column_total = jnp.sum(col_sum[...], axis=0, keepdims=True)
+    for i in range(PLANE):
+        col_mass[0:1, absolute(i)] = column_total[:, i * rows : (i + 1) * rows]
 
     mass = Gather(m_send, m_recv)
     mass.add("c", lambda mine_, send, recv: copy(row_mass, row_in, send, recv, sibling))
@@ -281,45 +346,47 @@
     mass.finish()
     row_mass[...] = 1.0 / jnp.sum(row_ins[...], axis=0)
     col_mass[...] = 1.0 / jnp.sum(col_ins2[...], axis=0)
+    for i in range(PLANE):
+        col_part[0:1, i * rows : (i + 1) * rows] = col_mass[0:1, absolute(i)]
 
     def pair_copy(n):
         return copy(sib_out.at[n], sib_in.at[n], s_send.at[n], s_recv.at[n], sibling)
 
-    def run_copy(s, m, h):
-        here = pl.ds(h * half, half)
-        at = (s * 4 + m) * 2 + h
+    def run_copy(s, m, q):
+        here = pl.ds(q * quarter, quarter)
+        at = (s * 4 + m) * 4 + q
         return copy(
             run_out.at[s * 4 + m, here], run_in.at[s * 4 + m, here], r_send.at[at], r_recv.at[at], z_mate(2 * s - 1)
         )
 
-    run_in[4, half:rows, :] = jnp.zeros((half, embed), HALF)
-    run_in[0, 0:half, :] = jnp.zeros((half, embed), HALF)
-
-    def link(i):
-        m, s = (i + 1) // 2, i % 2
-        pair_copy(i).wait_recv()
-        for h in (0, 1):
-            here = slice(h * half, (h + 1) * half)
-
-            @pl.when(jnp.logical_or(m > 1, s == 1 - h))
-            def _():
-                run_copy(s, m - 1, h).wait_recv()
-
-            total = mine[i, here, :] + sib_in[i, here, :].astype(SINGLE) + run_in[s * 4 + m - 1, here, :].astype(SINGLE)
-            run_out[s * 4 + m, here, :] = total.astype(HALF)
-            run_copy(s, m, h).start()
+    def comes(s, m, q):
+        return m > 0 or q // 2 == 1 - s
+
+    def link(m):
+        for s in (0, 1):
+            pair_copy(2 * m + 1 + s).wait_recv()
+        for q in range(4):
+            here = slice(q * quarter, (q + 1) * quarter)
+            for s in (1, 0):
+                n = 2 * m + 1 + s
+                total = mine[n, here, :] + sib_in[n, here, :].astype(SINGLE)
+                if comes(s, m, q):
+                    run_copy(s, m, q).wait_recv()
+                    total = total + run_in[s * 4 + m, here, :].astype(SINGLE)
+                run_out[s * 4 + m + 1, here, :] = total.astype(HALF)
+                run_copy(s, m + 1, q).start()
 
     def pull_step(n, carry):
-        o = (4 - (n + 1) // 2) * (2 * (n % 2) - 1)
-        i = (z + o + Z) % Z
-        here = span(i * chunk, chunk)
+        j = Z - 1 - n
+        i = (z + (j + 1) // 2 * (2 * (j % 2) - 1) + Z) % Z
+        here = span(j * chunk, chunk)
         inverse = to_column(row_mass[pl.ds(i, 1), :])
         total = jnp.zeros((chunk, 1), SINGLE)
         moved = jnp.zeros((chunk, embed), SINGLE)
         width = 2 * chunk
         for j in range(PLANE * rows // width):
             there = slice(j * width, (j + 1) * width)
-            pair = ((inverse + col_mass[0:1, there]) * tile[here, there]).astype(HALF)
+            pair = ((inverse + col_part[0:1, there]) * tile[here, there]).astype(HALF)
             total = total + jnp.sum(pair.astype(SINGLE), axis=1, keepdims=True)
             moved = moved + jnp.dot(pair, planes[there, :], preferred_element_type=SINGLE)
         pull = lines[here, :].astype(SINGLE) * total - moved
@@ -333,21 +400,24 @@
             far = (mine[0] + sib_in[0].astype(SINGLE)).astype(HALF)
             run_out[4] = far
             run_out[0] = far
-            run_copy(1, 0, 0).start()
-            run_copy(0, 0, 1).start()
-
-        @pl.when(n >= 2)
-        def _():
-            link(n - 1)
+            for q in range(4):
+                run_copy(1 - q // 2, 0, q).start()
+
+        for m, after in ((0, 3), (1, 6), (2, 7)):
+
+            @pl.when(n == after)
+            def _():
+                link(m)
 
         return carry
 
     lax.fori_loop(0, Z, pull_step, 0)
     pair_copy(Z - 1).wait_recv()
     pull = mine[Z - 1] + sib_in[Z - 1].astype(SINGLE)
-    for s in (0, 1):
-        for h in (0, 1):
-            run_copy(s, 3, h).wait_recv()
+    for q in range(4):
+        for s in (1, 0):
+            run_copy(s, 3, q).wait_recv()
+    for s in (1, 0):
         pull = pull + run_in[s * 4 + 3].astype(SINGLE)
     gradient = jnp.where(live > 0.5, 0.5 * pull, 0.0).astype(HALF)
 
@@ -355,7 +425,9 @@
     terms = Gather(w_send, w_recv)
     terms.add("c", lambda mine_, send, recv: copy(gradients.at[span(0, rows)], gradients.at[span(rows, rows)], send, recv, sibling))
     terms.start("c")
-    grad_embed[...] = gradient
+    embed_out[...] = gradient
+    stores = [pltpu.make_async_copy(embed_out, grad_embed, store.at[0])]
+    stores[0].start()
     gather.wait("feats")
     split = embed // 2
     share = group // XH
@@ -407,7 +479,9 @@
             first_out[1, to_y, to_x * share : (to_x + 1) * share, :] = piece[:, split:embed]
     for d in range(1, X):
         terms.start(("first", 0, d), ("first", 1, d))
-    grad_feats[...] = nt(gradient, weight[...]).astype(HALF)
+    feats_out[...] = nt(gradient, weight[...]).astype(HALF)
+    stores.append(pltpu.make_async_copy(feats_out, grad_feats, store.at[1]))
+    stores[1].start()
     for table, at in ((0, x), (1, y)):
         first_in[table, at] = first_out[table, at]
         terms.wait(*[("first", table, d) for d in range(1, X)])
@@ -424,18 +498,34 @@
     terms.start(*[("third", d) for d in range(1, Z)])
     third_in[z] = third_out[z]
     terms.wait(*terms.made)
-    grad_weight[...] = jnp.sum(third_in[...], axis=0)
+    weight_out[...] = jnp.sum(third_in[...], axis=0)
+    stores.append(pltpu.make_async_copy(weight_out, grad_weight, store.at[2]))
+    stores[2].start()
 
     gather.finish()
     terms.finish()
     for n in range(Z):
         pair_copy(n).wait_send()
-    run_copy(1, 0, 0).wait_send()
-    run_copy(0, 0, 1).wait_send()
     for s in (0, 1):
-        for m in (1, 2, 3):
-            for h in (0, 1):
-                run_copy(s, m, h).wait_send()
+        for m in range(4):
+            for q in range(4):
+                if comes(s, m, q):
+                    run_copy(s, m, q).wait_send()
+    for one in stores:
+        one.wait()
+
+
+def place(*refs):
+    sources, targets, held, get, put = refs[0:3], refs[3:6], refs[6:9], refs[9], refs[10]
+    gets = [pltpu.make_async_copy(a, b, get.at[i]) for i, (a, b) in enumerate(zip(sources, held))]
+    puts = [pltpu.make_async_copy(a, b, put.at[i]) for i, (a, b) in enumerate(zip(held, targets))]
+    for one in gets:
+        one.start()
+    for one, other in zip(gets, puts):
+        one.wait()
+        other.start()
+    for one in puts:
+        one.wait()
 
 
 def local(feats, weight, valid):
@@ -443,7 +533,7 @@
     embed = weight.shape[1]
     frames = rows * LINE * PLANE
     out_rows = width // (LINE * PLANE)
-    vmem = pl.BlockSpec(memory_space=pltpu.VMEM)
+    hbm = pl.BlockSpec(memory_space=pl.ANY)
 
     def half(*shape):
         return pltpu.VMEM(shape, HALF)
@@ -456,17 +546,21 @@
 
     share = Z * out_rows
     columns = PLANE * rows
-    return pl.pallas_call(
+    shapes = (
+        jax.ShapeDtypeStruct((rows, embed), HALF),
+        jax.ShapeDtypeStruct((rows, width), HALF),
+        jax.ShapeDtypeStruct((out_rows, embed), SINGLE),
+    )
+    results = pl.pallas_call(
         functools.partial(kernel, band=float(embed // 4), scale=math.sqrt(width) / frames),
-        out_shape=(
-            jax.ShapeDtypeStruct((rows, embed), HALF),
-            jax.ShapeDtypeStruct((rows, width), HALF),
-            jax.ShapeDtypeStruct((out_rows, embed), SINGLE),
-        ),
-        in_specs=[vmem] * 3,
-        out_specs=(vmem,) * 3,
+        out_shape=shapes,
+        in_specs=[hbm] * 3,
+        out_specs=(hbm,) * 3,
         scratch_shapes=[
+            half(rows, width), half(width, embed), pltpu.VMEM((1, rows), jnp.int32),
+            half(rows, embed), half(rows, width), single(out_rows, embed),
             half(LINE * rows, embed), half(columns, embed), single(1, columns), single(LINE * rows, columns),
+            single(LINE * rows, 128), single(LINE * rows, 128), single(8, columns),
             single(Z, C * rows), single(Z, C * rows), single(Z, C * rows), single(Z, Z, C * rows),
             single(1, columns), single(X, 1, columns), single(1, columns), single(Y, 1, columns),
             single(Z, rows, embed), half(Z, rows, embed), half(Z, rows, embed),
@@ -476,11 +570,19 @@
             half(2, 4, share, embed // 2), half(2, 4, share, embed // 2),
             single(Z, out_rows, embed), single(Z, out_rows, embed),
         ]
-        + dma(64) + dma(14) + dma(Z) + dma(16) + dma(20),
+        + [pltpu.SemaphoreType.DMA((6,)), pltpu.SemaphoreType.DMA((3,))]
+        + dma(64) + dma(14) + dma(Z) + dma(32) + dma(20),
         compiler_params=pltpu.CompilerParams(
             collective_id=0, has_side_effects=True, vmem_limit_bytes=56 * 1024 * 1024
         ),
     )(feats, weight, valid.reshape(1, rows))
+    return pl.pallas_call(
+        place,
+        out_shape=shapes,
+        in_specs=[hbm] * 3,
+        out_specs=(hbm,) * 3,
+        scratch_shapes=[pltpu.VMEM(one.shape, one.dtype) for one in shapes] + dma(3),
+    )(*results)
 
 
 def solution(mesh):

time: 90 us -> 82.7 us (0.919)
  local copies, waits for them, and re-layouts: 4.77 us -> 0 us
  Pallas kernels: 84.4 us -> 81.9 us
    unnamed x3 -> x0, local copies, waits for them, and re-layouts: 4.77 us -> none
    pallas_call x1, Pallas kernels: 84.4 us -> 79.9 us  [local(): pl.pallas_call(functools.partial(kernel, band=float(embed // 4), scale=ma...]
    pallas_call x0 -> x1, Pallas kernels: none -> 1.96 us  [local(): pl.pallas_call(place, out_shape=shapes, in_specs=[hbm] * 3, out_specs=(hb...]
where the time goes in v3:
time: 82.7 us; the launch traced here: 82.5 us
  Pallas kernels  81.9 us (99%)
    pallas_call x1, Pallas kernels, local(): pl.pallas_call(functools.partial(kernel, band=float(embed // 4), scale=ma...  79.9 us
    pallas_call x1, Pallas kernels, local(): pl.pallas_call(place, out_shape=shapes, in_specs=[hbm] * 3, out_specs=(hb...  1.96 us

profile of v3, /device:TPU:1, one launch (start us, length us, event | category | flops | bytes accessed | tf_op | source)
XLA Modules:
  0.0 82.5 jit_solution(5038017498957485849)
XLA Ops:
  0.6 79.9 %shard_map.58 = (bf16[128,512]{1,0:T(8,128)(2,1)}, bf16[128,2048]{1,0:T(8,128)(2,1)}, f32[8,512]{1,0:T(8,128)}) custom-call(bf16[128,2048]{1,0:T(8,128)(2,1)} %feats_in.1, bf16[2048,512]{1,0:T(8,128)(2,1)} %weight_in.1, s32[1,128]{1,0:T(1,128)} %bitcast.1), custom_call_target="tpu_custom_call" | custom-call | tf_op jit(solution)/shard_map/pallas_call | solution.py:554
  80.6 2.0 %shard_map.59 = (bf16[128,512]{1,0:T(8,128)(2,1)}, bf16[128,2048]{1,0:T(8,128)(2,1)}, f32[8,512]{1,0:T(8,128)}) custom-call(bf16[128,512]{1,0:T(8,128)(2,1)} %get-tuple-element.6.refs_0_, bf16[128,2048]{1,0:T(8,128)(2,1)} %get-tuple-element.7.refs_1_, f32[8,512]{1,0:T(8,128)} %get-tuple-element.8.refs_2_), custom_call_target="tpu_custom_call" | custom-call | tf_op jit(solution)/shard_map/pallas_call | solution.py:579

commit v4 on v3

--- a/solution.py
+++ b/solution.py
@@ -88,7 +88,7 @@
     lines, planes, norms, tile, row_norm, row_sum, col_sum,
     row_mass, row_in, row_pair, row_ins, col_mass, col_ins, col_part, col_ins2,
     mine, sib_out, sib_in, run_out, run_in,
-    mixed, leaving, gradients, first_out, first_in, second_out, second_in, third_out, third_in,
+    mixed, leaving, turned, gradients, first_out, first_stop, first_in, second_out, second_in, third_out, third_in,
     load, store, g_send, g_recv, m_send, m_recv, s_send, s_recv, r_send, r_recv, w_send, w_recv,
     *, band, scale,
 ):
@@ -122,7 +122,6 @@
         loads.append(pltpu.make_async_copy(weight_in.at[part], weight.at[part], load.at[2 + i]))
     for one in loads:
         one.start()
-    col_sum[...] = jnp.zeros_like(col_sum)
     loads[0].wait()
     loads[1].wait()
 
@@ -144,13 +143,6 @@
     own = jnp.where(live > 0.5, embedding, away).astype(HALF)
     lines[span(k * rows, rows), :] = own
     planes[0:rows, :] = own
-    group = XH * Z * grad_weight.shape[0]
-    for g in range(Y * XL):
-        low, high = feats[:, 2 * g * group : (2 * g + 1) * group], feats[:, (2 * g + 1) * group : (2 * g + 2) * group]
-        here = slice(g * group, (g + 1) * group)
-        mixed[0:rows, here] = jnp.where(k == 0, low, high)
-        leaving[:, here] = jnp.where(k == 0, high, low)
-
     pl.semaphore_wait(barrier, len(friends))
 
     half, quarter = rows // 2, rows // 4
@@ -162,18 +154,19 @@
     def plane_at(dx, dy, start, n):
         return planes.at[pl.ds(plane_slot(dx, dy) * rows + start, n)]
 
-    def along_z(s, d, h):
-        def make(sender, send, recv):
-            source = line_at(-s * (d - 1), k, h * half, half)
-            return copy(source, line_at(-s * d, k, h * half, half), send, recv, z_mate(s))
+    def along_z(s, d, q):
+        at = (q if s == 1 else 3 - q) * quarter
+
+        def make(sender, send, recv):
+            source = line_at(-s * (d - 1), k, at, quarter)
+            return copy(source, line_at(-s * d, k, at, quarter), send, recv, z_mate(s))
 
         return make
 
     for s in (1, -1):
         for d in range(1, Z // 2 + 1):
-            for h in (0, 1):
-                if d < Z // 2 or h == (0 if s == 1 else 1):
-                    gather.add(("z", s, d, h), along_z(s, d, h), [("z", s, d - 1, h)] if d > 1 else [])
+            for q in range(4 if d < Z // 2 else 2):
+                gather.add(("z", s, d, q), along_z(s, d, q), [("z", s, d - 1, q)] if d > 1 else [])
 
     def across(o):
         def make(sender, send, recv):
@@ -186,9 +179,9 @@
         if o == 0:
             needs = []
         elif o == Z // 2:
-            needs = [("z", 1, o, 0), ("z", -1, o, 1)]
+            needs = [("z", s, o, q) for s in (1, -1) for q in (0, 1)]
         else:
-            needs = [("z", -1 if o > 0 else 1, abs(o), h) for h in (0, 1)]
+            needs = [("z", -1 if o > 0 else 1, abs(o), q) for q in range(4)]
         gather.add(("c", o), across(o), needs)
 
     def in_plane(axis, s, along, beside, start, n):
@@ -231,10 +224,22 @@
     gather.add("feats", swap_copy)
 
     both = (1, -1)
+    def pass_z(d, *pieces):
+        gather.start(*[("z", s, d, q) for q in pieces for s in both])
+
     gather.start(*[("x", s, "own", 0) for s in both], *[("y", s, "own", 1) for s in both])
-    gather.start(*[("z", s, 1, 0) for s in both])
+    pass_z(1, 0, 1)
     gather.start(*[("x", s, "own", 1) for s in both], *[("y", s, "own", 0) for s in both])
-    gather.start(*[("z", s, 1, 1) for s in both], ("c", 0), "feats")
+    pass_z(1, 2, 3)
+    gather.start(("c", 0))
+
+    group = XH * Z * grad_weight.shape[0]
+    for g in range(Y * XL):
+        low, high = feats[:, 2 * g * group : (2 * g + 1) * group], feats[:, (2 * g + 1) * group : (2 * g + 2) * group]
+        here = slice(g * group, (g + 1) * group)
+        mixed[0:rows, here] = jnp.where(k == 0, low, high)
+        leaving[:, here] = jnp.where(k == 0, high, low)
+    gather.start("feats")
 
     def norm_of(first, last):
         for i in range(first, last):
@@ -272,42 +277,40 @@
 
         lax.fori_loop(first_row, last_row, step, 0)
 
+    col_sum[...] = jnp.zeros_like(col_sum)
     norm_of(0, 1)
-    gather.start(*[("z", s, 2, 0) for s in both], ("x", 1, "far"), ("y", -1, "far"))
+    pass_z(2, 0)
+    gather.start(("x", 1, "far"), ("y", -1, "far"))
     gather.start(*[(axis, s, "side", t) for t in both for axis in "yx" for s in both])
-    gather.start(*[("z", s, 2, 1) for s in both], ("x", -1, "far"), ("y", 1, "far"), ("c", 1), ("c", -1))
+    pass_z(2, 1, 2, 3)
+    gather.start(("x", -1, "far"), ("y", 1, "far"), ("c", 1), ("c", -1))
     gather.wait(*[(axis, s, "own", g) for axis in "xy" for s in both for g in (0, 1)])
     norm_of(1, 5)
+    pass_z(3, 0, 1)
     gather.wait(("c", 0), ("c", 1), ("c", -1))
     work(0, 3, 0, 2)
-    gather.start(*[("z", s, 3, 0) for s in both])
+    pass_z(3, 2, 3)
+    gather.start(("c", 2), ("c", -2))
     gather.start(*[(axis, s, "across") for axis in "yx" for s in both])
+    pass_z(4, 0, 1)
     gather.start(*[(axis, s, "side far", t) for t in both for axis in "yx" for s in both])
-    gather.start(*[("z", s, 3, 1) for s in both], ("c", 2), ("c", -2))
     gather.wait(*[(axis, s, "far") for axis in "xy" for s in both])
     norm_of(5, 11)
     work(0, 3, 2, 5)
-    gather.start(("z", 1, 4, 0), ("z", -1, 4, 1))
     gather.start(*[(axis, s, "across far") for axis in "yx" for s in both])
+    gather.start(("c", 3), ("c", -3), ("c", 4))
     gather.wait(("c", 2), ("c", -2))
     work(3, 5, 0, 5)
-    gather.start(("c", 3), ("c", -3), ("c", 4))
     gather.wait(*[(axis, s, "side far", t) for t in both for axis in "yx" for s in both])
     norm_of(11, 15)
     work(0, 5, 5, 7)
     gather.wait(("c", 3), ("c", -3))
     work(5, 7, 0, 7)
-    gather.wait(*gather.made)
+    gather.wait(*[(axis, s, "across far") for axis in "xy" for s in both])
     norm_of(15, 16)
     work(0, 7, 7, 8)
+    gather.wait(*gather.made)
     work(7, 8, 0, 8)
-
-    def row_total(i, carry):
-        place = (z + (i + 1) // 2 * (2 * (i % 2) - 1) + Z) % Z
-        row_mass[pl.ds(place, 1), :] = to_row(jnp.sum(row_sum[span(i * chunk, chunk), :], axis=1, keepdims=True))
-        return carry
-
-    lax.fori_loop(0, Z, row_total, 0)
 
     def absolute(slot):
         dx, dy = AROUND[slot]
@@ -332,8 +335,16 @@
         mass.add(("y", d), direct(col_part, col_ins2, y_mate, Y, y, d))
     for d in range(1, Z):
         mass.add(("z", d), direct(row_pair, row_ins, z_mate, Z, z, d))
-    mass.start("c", *[("x", d) for d in range(1, X)])
+    mass.start(*[("x", d) for d in range(1, X)])
     col_ins[x] = col_mass[...]
+
+    def row_total(i, carry):
+        place = (z + (i + 1) // 2 * (2 * (i % 2) - 1) + Z) % Z
+        row_mass[pl.ds(place, 1), :] = to_row(jnp.sum(row_sum[span(i * chunk, chunk), :], axis=1, keepdims=True))
+        return carry
+
+    lax.fori_loop(0, Z, row_total, 0)
+    mass.start("c")
     mass.wait("c")
     row_pair[...] = row_mass[...] + row_in[...]
     mass.start(*[("z", d) for d in range(1, Z)])
@@ -342,6 +353,9 @@
     col_part[...] = jnp.sum(col_ins[...], axis=0)
     mass.start(*[("y", d) for d in range(1, Y)])
     col_ins2[y] = col_part[...]
+    for g in range(Y * XL):
+        here = slice(g * group, (g + 1) * group)
+        turned[here, :] = mixed[:, here].T
     mass.wait(*mass.made)
     mass.finish()
     row_mass[...] = 1.0 / jnp.sum(row_ins[...], axis=0)
@@ -413,18 +427,26 @@
 
     lax.fori_loop(0, Z, pull_step, 0)
     pair_copy(Z - 1).wait_recv()
-    pull = mine[Z - 1] + sib_in[Z - 1].astype(SINGLE)
+    terms = Gather(w_send, w_recv)
+
+    def swap_gradient(q):
+        def make(sender, send, recv):
+            source, target = gradients.at[pl.ds(q * quarter, quarter)], gradients.at[pl.ds(rows + q * quarter, quarter)]
+            return copy(source, target, send, recv, sibling)
+
+        return make
+
     for q in range(4):
+        here = slice(q * quarter, (q + 1) * quarter)
+        pull = mine[Z - 1, here, :] + sib_in[Z - 1, here, :].astype(SINGLE)
         for s in (1, 0):
             run_copy(s, 3, q).wait_recv()
-    for s in (1, 0):
-        pull = pull + run_in[s * 4 + 3].astype(SINGLE)
-    gradient = jnp.where(live > 0.5, 0.5 * pull, 0.0).astype(HALF)
-
-    gradients[0:rows, :] = gradient
-    terms = Gather(w_send, w_recv)
-    terms.add("c", lambda mine_, send, recv: copy(gradients.at[span(0, rows)], gradients.at[span(rows, rows)], send, recv, sibling))
-    terms.start("c")
+            pull = pull + run_in[s * 4 + 3, here, :].astype(SINGLE)
+        gradients[here, :] = jnp.where(live[here, :] > 0.5, 0.5 * pull, 0.0).astype(HALF)
+        terms.add(("c", q), swap_gradient(q))
+        terms.start(("c", q))
+    gradient = gradients[0:rows, :]
+
     embed_out[...] = gradient
     stores = [pltpu.make_async_copy(embed_out, grad_embed, store.at[0])]
     stores[0].start()
@@ -432,13 +454,20 @@
     split = embed // 2
     share = group // XH
 
-    def first(table, axis, mate, size, at, d):
-        def make(sender, send, recv):
-            return copy(
-                first_out.at[table, (at + d) % size],
-                first_in.at[table, at if sender else (at - d + size) % size],
-                send, recv, mate(d),
-            )
+    side = 2 * share
+
+    def first_copy(table, s, step):
+        mate, size, at = (x_mate, X, x) if table == 0 else (y_mate, Y, y)
+        near, far = (at + s + size) % size, (at + 2) % size
+        low = s == 1
+        way = 0 if s == 1 else 1
+        stepped, plain = pl.ds(0 if low else side, side), pl.ds(side if low else 0, side)
+
+        def make(sender, send, recv):
+            if step == 0:
+                return copy(first_out.at[table, far, stepped], first_stop.at[table, way], send, recv, mate(s))
+            rows_of = plain if step == 1 else stepped
+            return copy(first_out.at[table, near, rows_of], first_in.at[table, way, rows_of], send, recv, mate(s))
 
         return make
 
@@ -458,52 +487,33 @@
 
         return make
 
+    for table in (0, 1):
+        for s in both:
+            for step in range(3):
+                terms.add(("first", table, s, step), first_copy(table, s, step))
     for d in range(1, X):
-        terms.add(("first", 0, d), first(0, "x", x_mate, X, x, d))
         terms.add(("second", 1, d), second(1, x_mate, X, x, d))
     for d in range(1, Y):
-        terms.add(("first", 1, d), first(1, "y", y_mate, Y, y, d))
         terms.add(("second", 0, d), second(0, y_mate, Y, y, d))
     for d in range(1, Z):
         terms.add(("third", d), third(d))
 
-    terms.wait("c")
+    terms.wait(*[("c", q) for q in range(4)])
     both_gradients = gradients[...]
     for g in range(Y * XL):
         to_y, low = g // XL, g % XL
-        term = (tn(mixed[:, g * group : (g + 1) * group], both_gradients) * scale).astype(HALF)
+        term = (
+            jnp.dot(turned[g * group : (g + 1) * group, :], both_gradients, preferred_element_type=SINGLE) * scale
+        ).astype(HALF)
         for high in range(XH):
             to_x = high * XL + low
             piece = term[high * share : (high + 1) * share, :]
             first_out[0, to_x, to_y * share : (to_y + 1) * share, :] = piece[:, 0:split]
             first_out[1, to_y, to_x * share : (to_x + 1) * share, :] = piece[:, split:embed]
-    for d in range(1, X):
-        terms.start(("first", 0, d), ("first", 1, d))
+    for step in (0, 1):
+        terms.start(*[("first", table, s, step) for table in (0, 1) for s in both])
     feats_out[...] = nt(gradient, weight[...]).astype(HALF)
-    stores.append(pltpu.make_async_copy(feats_out, grad_feats, store.at[1]))
-    stores[1].start()
-    for table, at in ((0, x), (1, y)):
-        first_in[table, at] = first_out[table, at]
-        terms.wait(*[("first", table, d) for d in range(1, X)])
-        added = jnp.sum(first_in[table].astype(SINGLE), axis=0).astype(HALF)
-        for i in range(4):
-            second_out[table, i] = added[i * share : (i + 1) * share, :]
-        terms.start(*[("second", table, d) for d in range(1, X)])
-    for table, at in ((0, y), (1, x)):
-        second_in[table, at] = second_out[table, at]
-        terms.wait(*[("second", table, d) for d in range(1, X)])
-        added = jnp.sum(second_in[table].astype(SINGLE), axis=0)
-        for i in range(Z):
-            third_out[i, :, table * split : (table + 1) * split] = added[i * (share // Z) : (i + 1) * (share // Z), :]
-    terms.start(*[("third", d) for d in range(1, Z)])
-    third_in[z] = third_out[z]
-    terms.wait(*terms.made)
-    weight_out[...] = jnp.sum(third_in[...], axis=0)
-    stores.append(pltpu.make_async_copy(weight_out, grad_weight, store.at[2]))
-    stores[2].start()
-
     gather.finish()
-    terms.finish()
     for n in range(Z):
         pair_copy(n).wait_send()
     for s in (0, 1):
@@ -511,6 +521,41 @@
             for q in range(4):
                 if comes(s, m, q):
                     run_copy(s, m, q).wait_send()
+    stores.append(pltpu.make_async_copy(feats_out, grad_feats, store.at[1]))
+    stores[1].start()
+    for table, at in ((0, x), (1, y)):
+        for s in both:
+            terms.wait(("first", table, s, 0))
+            near, way = (at + s + 4) % 4, 0 if s == 1 else 1
+            here = slice(0, side) if s == 1 else slice(side, 2 * side)
+            passed = first_out[table, near, here].astype(SINGLE) + first_stop[table, way].astype(SINGLE)
+            first_out[table, near, here] = passed.astype(HALF)
+            terms.start(("first", table, s, 2))
+    for table, at in ((0, x), (1, y)):
+        terms.wait(*[("first", table, s, step) for s in both for step in (1, 2)])
+        added = first_out[table, at].astype(SINGLE)
+        added = (added + first_in[table, 0].astype(SINGLE) + first_in[table, 1].astype(SINGLE)).astype(HALF)
+        for i in range(4):
+            second_out[table, i] = added[i * share : (i + 1) * share, :]
+        terms.start(*[("second", table, d) for d in range(1, X)])
+    totals = []
+    for table, at in ((0, y), (1, x)):
+        second_in[table, at] = second_out[table, at]
+        terms.wait(*[("second", table, d) for d in range(1, X)])
+        totals.append(jnp.sum(second_in[table].astype(SINGLE), axis=0))
+    few = share // Z
+    for i in range(Z):
+        here = slice(i * few, (i + 1) * few)
+        third_out[i] = jnp.concatenate([total[here, :] for total in totals], axis=0).astype(HALF)
+    terms.start(*[("third", d) for d in range(1, Z)])
+    third_in[z] = third_out[z]
+    terms.wait(*terms.made)
+    summed = jnp.sum(third_in[...].astype(SINGLE), axis=0)
+    weight_out[...] = jnp.concatenate([summed[0:few, :], summed[few : 2 * few, :]], axis=1)
+    stores.append(pltpu.make_async_copy(weight_out, grad_weight, store.at[2]))
+    stores[2].start()
+
+    terms.finish()
     for one in stores:
         one.wait()
 
@@ -565,13 +610,13 @@
             single(1, columns), single(X, 1, columns), single(1, columns), single(Y, 1, columns),
             single(Z, rows, embed), half(Z, rows, embed), half(Z, rows, embed),
             half(8, rows, embed), half(8, rows, embed),
-            half(2 * rows, width // 2), half(rows, width // 2), half(2 * rows, embed),
-            half(2, 4, 4 * share, embed // 2), half(2, 4, 4 * share, embed // 2),
+            half(2 * rows, width // 2), half(rows, width // 2), half(width // 2, 2 * rows), half(2 * rows, embed),
+            half(2, 4, 4 * share, embed // 2), half(2, 2, 2 * share, embed // 2), half(2, 2, 4 * share, embed // 2),
             half(2, 4, share, embed // 2), half(2, 4, share, embed // 2),
-            single(Z, out_rows, embed), single(Z, out_rows, embed),
+            half(Z, 2 * out_rows, embed // 2), half(Z, 2 * out_rows, embed // 2),
         ]
         + [pltpu.SemaphoreType.DMA((6,)), pltpu.SemaphoreType.DMA((3,))]
-        + dma(64) + dma(14) + dma(Z) + dma(32) + dma(20),
+        + dma(80) + dma(14) + dma(Z) + dma(32) + dma(29),
         compiler_params=pltpu.CompilerParams(
             collective_id=0, has_side_effects=True, vmem_limit_bytes=56 * 1024 * 1024
         ),

time: 82.7 us -> 80.8 us (0.977)
  Pallas kernels: 81.9 us -> 80.1 us
    pallas_call x1, Pallas kernels: 79.9 us -> 78.1 us  [local(): pl.pallas_call(functools.partial(kernel, band=float(embed // 4), scale=ma...]
where the time goes in v4:
time: 80.8 us; the launch traced here: 80.7 us
  Pallas kernels  80.1 us (99%)
    pallas_call x1, Pallas kernels, local(): pl.pallas_call(functools.partial(kernel, band=float(embed // 4), scale=ma...  78.1 us
    pallas_call x1, Pallas kernels, local(): pl.pallas_call(place, out_shape=shapes, in_specs=[hbm] * 3, out_specs=(hb...  1.96 us

profile of v4, /device:TPU:1, one launch (start us, length us, event | category | flops | bytes accessed | tf_op | source)
XLA Modules:
  0.0 80.7 jit_solution(9774955026931161524)
XLA Ops:
  0.6 78.1 %shard_map.58 = (bf16[128,512]{1,0:T(8,128)(2,1)}, bf16[128,2048]{1,0:T(8,128)(2,1)}, f32[8,512]{1,0:T(8,128)}) custom-call(bf16[128,2048]{1,0:T(8,128)(2,1)} %feats_in.1, bf16[2048,512]{1,0:T(8,128)(2,1)} %weight_in.1, s32[1,128]{1,0:T(1,128)} %bitcast.1), custom_call_target="tpu_custom_call" | custom-call | tf_op jit(solution)/shard_map/pallas_call | solution.py:599
  78.7 2.0 %shard_map.59 = (bf16[128,512]{1,0:T(8,128)(2,1)}, bf16[128,2048]{1,0:T(8,128)(2,1)}, f32[8,512]{1,0:T(8,128)}) custom-call(bf16[128,512]{1,0:T(8,128)(2,1)} %get-tuple-element.6.refs_0_, bf16[128,2048]{1,0:T(8,128)(2,1)} %get-tuple-element.7.refs_1_, f32[8,512]{1,0:T(8,128)} %get-tuple-element.8.refs_2_), custom_call_target="tpu_custom_call" | custom-call | tf_op jit(solution)/shard_map/pallas_call | solution.py:624

commit v5 on v4

--- a/solution.py
+++ b/solution.py
@@ -85,7 +85,7 @@
     feats_in, weight_in, valid_in,
     grad_embed, grad_feats, grad_weight,
     feats, weight, valid, embed_out, feats_out, weight_out,
-    lines, planes, norms, tile, row_norm, row_sum, col_sum,
+    lines, planes, planes_t, norms, tile, row_norm, row_sum, col_sum,
     row_mass, row_in, row_pair, row_ins, col_mass, col_ins, col_part, col_ins2,
     mine, sib_out, sib_in, run_out, run_in,
     mixed, leaving, turned, gradients, first_out, first_stop, first_in, second_out, second_in, third_out, third_in,
@@ -244,6 +244,7 @@
     def norm_of(first, last):
         for i in range(first, last):
             here = slice(i * rows, (i + 1) * rows)
+            planes_t[:, here] = planes[here, :].T
             wide = planes[here, :].astype(SINGLE)
             norms[0:1, here] = to_row(jnp.sum(wide * wide, axis=1, keepdims=True))
 
@@ -266,7 +267,9 @@
             twice = block * 2
             for j in range(first_unit, last_unit):
                 there = slice(j * chunk, (j + 1) * chunk)
-                distance = (norm + norms[0:1, there]) - nt(twice, planes[there, :])
+                distance = (norm + norms[0:1, there]) - jnp.dot(
+                    twice, planes_t[:, there], preferred_element_type=SINGLE
+                )
                 value = jnp.exp2(distance * rate)
                 tile[here, there] = value
                 for p in range(chunk // 128):
@@ -345,6 +348,9 @@
 
     lax.fori_loop(0, Z, row_total, 0)
     mass.start("c")
+    for g in range(Y * XL):
+        here = slice(g * group, (g + 1) * group)
+        turned[here, :] = mixed[:, here].T
     mass.wait("c")
     row_pair[...] = row_mass[...] + row_in[...]
     mass.start(*[("z", d) for d in range(1, Z)])
@@ -353,9 +359,6 @@
     col_part[...] = jnp.sum(col_ins[...], axis=0)
     mass.start(*[("y", d) for d in range(1, Y)])
     col_ins2[y] = col_part[...]
-    for g in range(Y * XL):
-        here = slice(g * group, (g + 1) * group)
-        turned[here, :] = mixed[:, here].T
     mass.wait(*mass.made)
     mass.finish()
     row_mass[...] = 1.0 / jnp.sum(row_ins[...], axis=0)
@@ -456,16 +459,16 @@
 
     side = 2 * share
 
-    def first_copy(table, s, step):
+    def first_copy(table, s, step, p):
         mate, size, at = (x_mate, X, x) if table == 0 else (y_mate, Y, y)
         near, far = (at + s + size) % size, (at + 2) % size
         low = s == 1
         way = 0 if s == 1 else 1
-        stepped, plain = pl.ds(0 if low else side, side), pl.ds(side if low else 0, side)
+        stepped, plain = pl.ds((0 if low else side) + p * share, share), pl.ds(side if low else 0, side)
 
         def make(sender, send, recv):
             if step == 0:
-                return copy(first_out.at[table, far, stepped], first_stop.at[table, way], send, recv, mate(s))
+                return copy(first_out.at[table, far, stepped], first_stop.at[table, way, pl.ds(p * share, share)], send, recv, mate(s))
             rows_of = plain if step == 1 else stepped
             return copy(first_out.at[table, near, rows_of], first_in.at[table, way, rows_of], send, recv, mate(s))
 
@@ -490,7 +493,8 @@
     for table in (0, 1):
         for s in both:
             for step in range(3):
-                terms.add(("first", table, s, step), first_copy(table, s, step))
+                for p in range(1 if step == 1 else 2):
+                    terms.add(("first", table, s, step, p), first_copy(table, s, step, p))
     for d in range(1, X):
         terms.add(("second", 1, d), second(1, x_mate, X, x, d))
     for d in range(1, Y):
@@ -510,8 +514,8 @@
             piece = term[high * share : (high + 1) * share, :]
             first_out[0, to_x, to_y * share : (to_y + 1) * share, :] = piece[:, 0:split]
             first_out[1, to_y, to_x * share : (to_x + 1) * share, :] = piece[:, split:embed]
-    for step in (0, 1):
-        terms.start(*[("first", table, s, step) for table in (0, 1) for s in both])
+    for step, p in ((0, 0), (0, 1), (1, 0)):
+        terms.start(*[("first", table, s, step, p) for table in (0, 1) for s in both])
     feats_out[...] = nt(gradient, weight[...]).astype(HALF)
     gather.finish()
     for n in range(Z):
@@ -523,16 +527,17 @@
                     run_copy(s, m, q).wait_send()
     stores.append(pltpu.make_async_copy(feats_out, grad_feats, store.at[1]))
     stores[1].start()
+    for p, table, s in [(p, table, s) for p in (0, 1) for table in (0, 1) for s in both]:
+        terms.wait(("first", table, s, 0, p))
+        near, way = ((x if table == 0 else y) + s + 4) % 4, 0 if s == 1 else 1
+        start = (0 if s == 1 else side) + p * share
+        here = slice(start, start + share)
+        passed = first_out[table, near, here].astype(SINGLE)
+        passed = passed + first_stop[table, way, p * share : (p + 1) * share].astype(SINGLE)
+        first_out[table, near, here] = passed.astype(HALF)
+        terms.start(("first", table, s, 2, p))
     for table, at in ((0, x), (1, y)):
-        for s in both:
-            terms.wait(("first", table, s, 0))
-            near, way = (at + s + 4) % 4, 0 if s == 1 else 1
-            here = slice(0, side) if s == 1 else slice(side, 2 * side)
-            passed = first_out[table, near, here].astype(SINGLE) + first_stop[table, way].astype(SINGLE)
-            first_out[table, near, here] = passed.astype(HALF)
-            terms.start(("first", table, s, 2))
-    for table, at in ((0, x), (1, y)):
-        terms.wait(*[("first", table, s, step) for s in both for step in (1, 2)])
+        terms.wait(*[("first", table, s, step, p) for s in both for step, p in ((1, 0), (2, 0), (2, 1))])
         added = first_out[table, at].astype(SINGLE)
         added = (added + first_in[table, 0].astype(SINGLE) + first_in[table, 1].astype(SINGLE)).astype(HALF)
         for i in range(4):
@@ -604,7 +609,7 @@
         scratch_shapes=[
             half(rows, width), half(width, embed), pltpu.VMEM((1, rows), jnp.int32),
             half(rows, embed), half(rows, width), single(out_rows, embed),
-            half(LINE * rows, embed), half(columns, embed), single(1, columns), single(LINE * rows, columns),
+            half(LINE * rows, embed), half(columns, embed), half(embed, columns), single(1, columns), single(LINE * rows, columns),
             single(LINE * rows, 128), single(LINE * rows, 128), single(8, columns),
             single(Z, C * rows), single(Z, C * rows), single(Z, C * rows), single(Z, Z, C * rows),
             single(1, columns), single(X, 1, columns), single(1, columns), single(Y, 1, columns),
@@ -616,7 +621,7 @@
             half(Z, 2 * out_rows, embed // 2), half(Z, 2 * out_rows, embed // 2),
         ]
         + [pltpu.SemaphoreType.DMA((6,)), pltpu.SemaphoreType.DMA((3,))]
-        + dma(80) + dma(14) + dma(Z) + dma(32) + dma(29),
+        + dma(80) + dma(14) + dma(Z) + dma(32) + dma(37),
         compiler_params=pltpu.CompilerParams(
             collective_id=0, has_side_effects=True, vmem_limit_bytes=56 * 1024 * 1024
         ),

time: 80.8 us -> 80.2 us (level)
  no operation moved by 1% of the time
where the time goes in v5:
time: 80.2 us; the launch traced here: 80 us
  Pallas kernels  79.4 us (99%)
    pallas_call x1, Pallas kernels, local(): pl.pallas_call(functools.partial(kernel, band=float(embed // 4), scale=ma...  77.4 us
    pallas_call x1, Pallas kernels, local(): pl.pallas_call(place, out_shape=shapes, in_specs=[hbm] * 3, out_specs=(hb...  1.96 us

profile of v5, /device:TPU:1, one launch (start us, length us, event | category | flops | bytes accessed | tf_op | source)
XLA Modules:
  0.0 80.0 jit_solution(9770507172784514108)
XLA Ops:
  0.6 77.4 %shard_map.58 = (bf16[128,512]{1,0:T(8,128)(2,1)}, bf16[128,2048]{1,0:T(8,128)(2,1)}, f32[8,512]{1,0:T(8,128)}) custom-call(bf16[128,2048]{1,0:T(8,128)(2,1)} %feats_in.1, bf16[2048,512]{1,0:T(8,128)(2,1)} %weight_in.1, s32[1,128]{1,0:T(1,128)} %bitcast.1), custom_call_target="tpu_custom_call" | custom-call | tf_op jit(solution)/shard_map/pallas_call | solution.py:604
  78.1 2.0 %shard_map.59 = (bf16[128,512]{1,0:T(8,128)(2,1)}, bf16[128,2048]{1,0:T(8,128)(2,1)}, f32[8,512]{1,0:T(8,128)}) custom-call(bf16[128,512]{1,0:T(8,128)(2,1)} %get-tuple-element.6.refs_0_, bf16[128,2048]{1,0:T(8,128)(2,1)} %get-tuple-element.7.refs_1_, f32[8,512]{1,0:T(8,128)} %get-tuple-element.8.refs_2_), custom_call_target="tpu_custom_call" | custom-call | tf_op jit(solution)/shard_map/pallas_call | solution.py:629

commit v6 on v5

--- a/solution.py
+++ b/solution.py
@@ -14,6 +14,7 @@
 LINE = Z * C
 PLANE = X * Y
 FAR = 2.0**60
+FARTHEST = (4, 3, 5, 2, 6, 1, 7)
 ALONG = (0, 1, -1, 2, -2, 3, -3, 4)
 AROUND = (
     (0, 0), (1, 0), (-1, 0), (0, 1), (0, -1), (2, 0), (0, 2), (1, 1), (-1, 1), (1, -1), (-1, -1),
@@ -338,7 +339,7 @@
         mass.add(("y", d), direct(col_part, col_ins2, y_mate, Y, y, d))
     for d in range(1, Z):
         mass.add(("z", d), direct(row_pair, row_ins, z_mate, Z, z, d))
-    mass.start(*[("x", d) for d in range(1, X)])
+    mass.start(*[("x", d) for d in (2, 1, 3)])
     col_ins[x] = col_mass[...]
 
     def row_total(i, carry):
@@ -353,11 +354,11 @@
         turned[here, :] = mixed[:, here].T
     mass.wait("c")
     row_pair[...] = row_mass[...] + row_in[...]
-    mass.start(*[("z", d) for d in range(1, Z)])
+    mass.start(*[("z", d) for d in FARTHEST])
     row_ins[z] = row_pair[...]
     mass.wait(*[("x", d) for d in range(1, X)])
     col_part[...] = jnp.sum(col_ins[...], axis=0)
-    mass.start(*[("y", d) for d in range(1, Y)])
+    mass.start(*[("y", d) for d in (2, 1, 3)])
     col_ins2[y] = col_part[...]
     mass.wait(*mass.made)
     mass.finish()
@@ -542,7 +543,7 @@
         added = (added + first_in[table, 0].astype(SINGLE) + first_in[table, 1].astype(SINGLE)).astype(HALF)
         for i in range(4):
             second_out[table, i] = added[i * share : (i + 1) * share, :]
-        terms.start(*[("second", table, d) for d in range(1, X)])
+        terms.start(*[("second", table, d) for d in (2, 1, 3)])
     totals = []
     for table, at in ((0, y), (1, x)):
         second_in[table, at] = second_out[table, at]
@@ -552,7 +553,7 @@
     for i in range(Z):
         here = slice(i * few, (i + 1) * few)
         third_out[i] = jnp.concatenate([total[here, :] for total in totals], axis=0).astype(HALF)
-    terms.start(*[("third", d) for d in range(1, Z)])
+    terms.start(*[("third", d) for d in FARTHEST])
     third_in[z] = third_out[z]
     terms.wait(*terms.made)
     summed = jnp.sum(third_in[...].astype(SINGLE), axis=0)

time: 80.2 us -> 79.7 us (level)
  no operation moved by 1% of the time
where the time goes in v6:
time: 79.7 us; the launch traced here: 79.5 us
  Pallas kernels  78.9 us (99%)
    pallas_call x1, Pallas kernels, local(): pl.pallas_call(functools.partial(kernel, band=float(embed // 4), scale=ma...  76.9 us
    pallas_call x1, Pallas kernels, local(): pl.pallas_call(place, out_shape=shapes, in_specs=[hbm] * 3, out_specs=(hb...  1.96 us

profile of v6, /device:TPU:1, one launch (start us, length us, event | category | flops | bytes accessed | tf_op | source)
XLA Modules:
  0.0 79.5 jit_solution(11927648277872152316)
XLA Ops:
  0.6 76.9 %shard_map.58 = (bf16[128,512]{1,0:T(8,128)(2,1)}, bf16[128,2048]{1,0:T(8,128)(2,1)}, f32[8,512]{1,0:T(8,128)}) custom-call(bf16[128,2048]{1,0:T(8,128)(2,1)} %feats_in.1, bf16[2048,512]{1,0:T(8,128)(2,1)} %weight_in.1, s32[1,128]{1,0:T(1,128)} %bitcast.1), custom_call_target="tpu_custom_call" | custom-call | tf_op jit(solution)/shard_map/pallas_call | solution.py:605
  77.6 2.0 %shard_map.59 = (bf16[128,512]{1,0:T(8,128)(2,1)}, bf16[128,2048]{1,0:T(8,128)(2,1)}, f32[8,512]{1,0:T(8,128)}) custom-call(bf16[128,512]{1,0:T(8,128)(2,1)} %get-tuple-element.6.refs_0_, bf16[128,2048]{1,0:T(8,128)(2,1)} %get-tuple-element.7.refs_1_, f32[8,512]{1,0:T(8,128)} %get-tuple-element.8.refs_2_), custom_call_target="tpu_custom_call" | custom-call | tf_op jit(solution)/shard_map/pallas_call | solution.py:630
